TPU v7x, 32 devices: a whole 2x2x4 slice. The times are simulated.
32 devices in a mesh: dp: 16 (over z, x, core), sp: 2 (over y).
Axes of the slice: x: 2, y: 2, z: 4, core: 2. Of those that a mesh axis runs over, the one named last changes fastest.
Arguments:
- vision: bfloat16 [16, 128, 8192], P('dp', None, 'sp'), may hold values from -6 to 6
- key_projection_weight: bfloat16 [8192, 1024], P(('sp', 'dp')), may hold values from -0.0625 to 0.0625
- value_projection_weight: bfloat16 [8192, 1024], P(('sp', 'dp')), may hold values from -0.0625 to 0.0625
- key_gain: float32 [128], replicated, may hold values from 0.1 to 1.9
- queries: bfloat16 [16, 256, 4096], P('dp', 'sp'), may hold values from -40 to 40
- out_grad: bfloat16 [16, 256, 4096], P('dp', 'sp'), may hold values from -6 to 6
- image_ids: int32 [16, 16], P('dp'), may hold values from 0 to 15
- image_counts: int32 [16], P('dp'), may hold values from 4 to 16
- image_starts: int32 [16, 16], P('dp'), may hold values from 0 to 255
Outputs:
- attended: bfloat16 [16, 256, 4096], P('dp', 'sp')
- grad_queries: bfloat16 [16, 256, 4096], P('dp', 'sp')
- grad_wkey: float32 [8192, 1024], P(('sp', 'dp'))
- grad_wvalue: float32 [8192, 1024], P(('sp', 'dp'))
Inputs may be any that keep to these rules, and one draw needn't show every extreme that they name: `image_starts`: slot 0 is seen by every token whatever its start.
All inputs are finite; a program needn't handle non-finite values.
Results may differ from a plain program's by a relative error of at most 0.015.
The roundings to bfloat16 on the way count: a program that leaves them out, or rounds other values in their place, can miss the bound.
Values may be sent and summed in bfloat16 or wider, within the bound.
No kernel may reach another device: no remote copies, remote signals or barrier semaphores. Data moves between devices by JAX's collectives and lax.ppermute only.
A program may use at most 128 MiB of HBM per device.

v0:
```python
import math

import jax
import jax.numpy as jnp
from jax import lax
from jax.sharding import PartitionSpec as P

KEY_VALUE_HEADS = 8
HEAD_SIZE = 128


norm_epsilon = 1e-05


def key_norm(key_before_projection, key_gain):
    mean_square = jnp.mean(key_before_projection * key_before_projection, axis=-1, keepdims=True)
    return key_before_projection * lax.rsqrt(mean_square + norm_epsilon) * key_gain


def visibility(row_sum_total, starts, image_count, image_tokens):
    key_slot = jnp.arange(starts.shape[0] * image_tokens, dtype=jnp.int32) // image_tokens
    slot_start = jnp.repeat(starts, image_tokens)
    position = jnp.arange(row_sum_total, dtype=jnp.int32)[:, None]
    return (key_slot[None, :] < image_count) & (
        (position >= slot_start[None, :]) | (key_slot[None, :] == 0)
    )


def head_pass(query_head, grad_head, key_head, value_head, visible):
    score_scale = 1.0 / math.sqrt(query_head.shape[-1])
    scores = jnp.dot(query_head, key_head.T, preferred_element_type=jnp.float32) * score_scale
    scores = jnp.where(visible, scores, -1e30)
    row_max = jnp.max(scores, axis=-1, keepdims=True)
    weights = jnp.exp(scores - row_max)
    prob_rows = weights / jnp.sum(weights, axis=-1, keepdims=True)
    probs_low = prob_rows.astype(jnp.bfloat16)
    attended = jnp.dot(probs_low, value_head, preferred_element_type=jnp.float32).astype(
        jnp.bfloat16
    )
    grad_probs = jnp.dot(grad_head, value_head.T, preferred_element_type=jnp.float32)
    row_delta = jnp.sum(
        grad_head.astype(jnp.float32) * attended.astype(jnp.float32), axis=-1, keepdims=True
    )
    grad_scores = (prob_rows * (grad_probs - row_delta) * score_scale).astype(jnp.bfloat16)
    grad_query = jnp.dot(grad_scores, key_head, preferred_element_type=jnp.float32).astype(
        jnp.bfloat16
    )
    key_gradient = jnp.dot(grad_scores.T, query_head, preferred_element_type=jnp.float32)
    value_gradient = jnp.dot(probs_low.T, grad_head, preferred_element_type=jnp.float32)
    return (attended, grad_query, key_gradient, value_gradient)


def document_pass(query_rows, grad_rows, key_heads, value_heads, visible):
    row_sum_total = query_rows.shape[0]
    query_heads = query_rows.shape[1] // HEAD_SIZE
    kv_heads = key_heads.shape[0]
    group_size = query_heads // kv_heads
    query_split = query_rows.reshape(row_sum_total, query_heads, HEAD_SIZE).transpose(1, 0, 2)
    grad_split = grad_rows.reshape(row_sum_total, query_heads, HEAD_SIZE).transpose(1, 0, 2)

    def per_head(head_index):
        kv_index = head_index // group_size
        return head_pass(
            query_split[head_index],
            grad_split[head_index],
            key_heads[kv_index],
            value_heads[kv_index],
            visible,
        )

    attended, grad_query, key_gradient, value_gradient = lax.map(
        per_head, jnp.arange(query_heads, dtype=jnp.int32)
    )
    attended = attended.transpose(1, 0, 2).reshape(row_sum_total, query_heads * HEAD_SIZE)
    grad_query = grad_query.transpose(1, 0, 2).reshape(row_sum_total, query_heads * HEAD_SIZE)
    key_total = key_heads.shape[1]
    key_gradient = key_gradient.reshape(kv_heads, group_size, key_total, HEAD_SIZE).sum(axis=1)
    value_gradient = value_gradient.reshape(kv_heads, group_size, key_total, HEAD_SIZE).sum(axis=1)
    return (attended, grad_query, key_gradient, value_gradient)


def shards(
    vision,
    key_projection_weight,
    value_projection_weight,
    key_gain,
    queries,
    out_grad,
    image_ids,
    image_counts,
    image_starts,
):
    sequence_split_total = lax.axis_size("sp")
    image_local, image_tokens, feature_cols = vision.shape
    row_sum_total = image_local * image_tokens
    local_key_value = KEY_VALUE_HEADS // sequence_split_total
    picture_rows = vision.reshape(row_sum_total, feature_cols)
    block_key, block_value = (
        lax.all_gather(key_projection_weight, "dp", axis=0, tiled=True),
        lax.all_gather(value_projection_weight, "dp", axis=0, tiled=True),
    )
    full_key, full_value = (
        lax.all_to_all(block_key, "sp", split_axis=1, concat_axis=0, tiled=True),
        lax.all_to_all(block_value, "sp", split_axis=1, concat_axis=0, tiled=True),
    )
    whole_vision = lax.all_gather(vision, "sp", axis=2, tiled=True).reshape(row_sum_total, -1)
    key_before_projection = jnp.dot(
        whole_vision, full_key, preferred_element_type=jnp.float32
    ).reshape(row_sum_total, local_key_value, HEAD_SIZE)
    value_before_projection = jnp.dot(
        whole_vision, full_value, preferred_element_type=jnp.float32
    ).reshape(row_sum_total, local_key_value, HEAD_SIZE)
    keys_low = key_norm(key_before_projection, key_gain).astype(jnp.bfloat16)
    own_pairs = jnp.stack((keys_low, value_before_projection.astype(jnp.bfloat16)), axis=2).reshape(
        image_local, image_tokens, local_key_value, 2, HEAD_SIZE
    )
    every_pair = lax.all_gather(own_pairs, "dp", axis=0, tiled=True)
    image_total = every_pair.shape[0]
    query_rows, grad_rows = (
        lax.all_to_all(queries, "sp", split_axis=2, concat_axis=1, tiled=True),
        lax.all_to_all(out_grad, "sp", split_axis=2, concat_axis=1, tiled=True),
    )
    query_rows = query_rows[0]
    grad_rows = grad_rows[0]
    document_index = image_ids[0]
    slot_count = document_index.shape[0]
    picked = every_pair[document_index]
    slotted_keys = (
        picked[:, :, :, 0]
        .reshape(slot_count * image_tokens, local_key_value, HEAD_SIZE)
        .transpose(1, 0, 2)
    )
    slotted_values = (
        picked[:, :, :, 1]
        .reshape(slot_count * image_tokens, local_key_value, HEAD_SIZE)
        .transpose(1, 0, 2)
    )
    visible = visibility(query_rows.shape[0], image_starts[0], image_counts[0], image_tokens)
    attended, grad_query, key_gradient, value_gradient = document_pass(
        query_rows, grad_rows, slotted_keys, slotted_values, visible
    )
    attended_output, output_gradient = (
        lax.all_to_all(attended[None], "sp", split_axis=1, concat_axis=2, tiled=True),
        lax.all_to_all(grad_query[None], "sp", split_axis=1, concat_axis=2, tiled=True),
    )
    slot_gradients = jnp.stack((key_gradient, value_gradient), axis=1).reshape(
        local_key_value, 2, slot_count, image_tokens, HEAD_SIZE
    )
    selector = (
        document_index[None, :] == jnp.arange(image_total, dtype=jnp.int32)[:, None]
    ).astype(jnp.float32)
    image_gradients = jnp.einsum(
        "es,hcstd->ethcd", selector, slot_gradients, precision=lax.Precision.HIGHEST
    )
    owned_grads = lax.psum_scatter(image_gradients, "dp", scatter_dimension=0, tiled=True).reshape(
        row_sum_total, local_key_value, 2, HEAD_SIZE
    )
    unused_out, norm_back = jax.vjp(
        lambda pre_norm: key_norm(pre_norm, key_gain), key_before_projection
    )
    key_backward_pass = norm_back(owned_grads[:, :, 0])[0]
    grads_low = jnp.stack((key_backward_pass, owned_grads[:, :, 1]), axis=2).astype(jnp.bfloat16)
    every_head = lax.all_gather(grads_low, "sp", axis=1, tiled=True)
    joined = jnp.concatenate(
        (
            every_head[:, :, 0].reshape(row_sum_total, KEY_VALUE_HEADS * HEAD_SIZE),
            every_head[:, :, 1].reshape(row_sum_total, KEY_VALUE_HEADS * HEAD_SIZE),
        ),
        axis=1,
    )
    weight_portion = lax.psum_scatter(
        lax.dot_general(
            picture_rows, joined, (((0,), (0,)), ((), ())), preferred_element_type=jnp.float32
        ).astype(jnp.bfloat16),
        "dp",
        scatter_dimension=0,
        tiled=True,
    ).astype(jnp.float32)
    return (
        attended_output,
        output_gradient,
        weight_portion[:, : KEY_VALUE_HEADS * HEAD_SIZE],
        weight_portion[:, KEY_VALUE_HEADS * HEAD_SIZE :],
    )


def solution(mesh):
    return jax.shard_map(
        shards,
        mesh=mesh,
        in_specs=(
            P("dp", None, "sp"),
            P(("sp", "dp"), None),
            P(("sp", "dp"), None),
            P(),
            P("dp", "sp", None),
            P("dp", "sp", None),
            P("dp", None),
            P("dp"),
            P("dp", None),
        ),
        out_specs=(
            P("dp", "sp", None),
            P("dp", "sp", None),
            P(("sp", "dp"), None),
            P(("sp", "dp"), None),
        ),
        check_vma=False,
    )
```

profile of v0, /device:TPU:0, one launch (start us, length us, event | category | flops | bytes accessed | tf_op | source)
XLA Modules:
  0.0 1099.6 jit_solution(11303762490977727077)
XLA Ops:
  12.2 80.2 %all-gather.8.cloned.1.call-done = bf16[4096,1024]{0,1:T(8,128)(2,1)} async-done(((bf16[256,1024]{0,1:T(8,128)(2,1)}), bf16[4096,1024]{0,1:T(8,128)(2,1)}) %all-gather.8.cloned.1.call-update) | async-done | bytes 8388624 | tf_op jit(solution)/shard_map/all_gather | solution.py:99
  92.4 12.1 %copy.115 = bf16[4096,2,512]{2,0,1:T(8,128)(2,1)} copy(bf16[4096,2,512]{0,2,1:T(8,128)(2,1)} %bitcast.211) | data formatting | bytes 16777216 | tf_op jit(solution)/shard_map/all_to_all | solution.py:103
  104.5 7.0 all-to-all-start.1
  111.5 60.0 %all-gather.10.cloned.1.call-done = bf16[4096,1024]{0,1:T(8,128)(2,1)} async-done(((bf16[256,1024]{0,1:T(8,128)(2,1)}), bf16[4096,1024]{0,1:T(8,128)(2,1)}) %all-gather.10.cloned.1.call-update) | async-done | bytes 8388624 | tf_op jit(solution)/shard_map/all_gather | solution.py:100
  171.4 12.0 %copy.118 = bf16[4096,2,512]{2,0,1:T(8,128)(2,1)} copy(bf16[4096,2,512]{0,2,1:T(8,128)(2,1)} %bitcast.212) | data formatting | bytes 16777216 | tf_op jit(solution)/shard_map/all_to_all | solution.py:104
  183.4 21.0 %all-to-all-done.1 = bf16[4096,2,512]{2,0,1:T(8,128)(2,1)} async-done(((bf16[4096,2,512]{2,0,1:T(8,128)(2,1)}), bf16[4096,2,512]{2,0,1:T(8,128)(2,1)}, u32[]{:S(2)}, u32[]{:S(2)}) %all-to-all-start.1) | async-done | bytes 8388640 | tf_op jit(solution)/shard_map/all_to_all | solution.py:103
  204.5 6.9 all-to-all-start.2
  212.0 12.0 %copy.116 = bf16[8192,512]{0,1:T(8,128)(2,1)} copy(bf16[8192,512]{1,0:T(8,128)(2,1)} %bitcast.6) | data formatting | bytes 16777216 | tf_op jit(solution)/shard_map/all_to_all | solution.py:103
  224.0 43.9 %all-gather.6.cloned.1.call-done = bf16[1,128,8192]{2,1,0:T(8,128)(2,1)} async-done(((bf16[1,128,4096]{2,1,0:T(8,128)(2,1)}), bf16[1,128,8192]{2,1,0:T(8,128)(2,1)}) %all-gather.6.cloned.1.call-update) | async-done | bytes 2097168 | tf_op jit(solution)/shard_map/all_gather | solution.py:106
  267.9 6.4 multiply_reduce_fusion.2
  274.3 51.8 %all-to-all-done.2 = bf16[4096,2,512]{2,0,1:T(8,128)(2,1)} async-done(((bf16[4096,2,512]{2,0,1:T(8,128)(2,1)}), bf16[4096,2,512]{2,0,1:T(8,128)(2,1)}, u32[]{:S(2)}, u32[]{:S(2)}) %all-to-all-start.2) | async-done | bytes 8388640 | tf_op jit(solution)/shard_map/all_to_all | solution.py:104
  326.1 12.0 %copy.119 = bf16[8192,512]{0,1:T(8,128)(2,1)} copy(bf16[8192,512]{1,0:T(8,128)(2,1)} %bitcast.12) | data formatting | bytes 16777216 | tf_op jit(solution)/shard_map/all_to_all | solution.py:104
  338.2 5.8 fusion.50
  344.8 2.8 copy.112
  348.2 22.3 %reduce = bf16[4096,128]{1,0:T(8,128)(2,1)S(1)} reduce(bf16[4096,1,128]{2,1,0:T(2,128)(2,1)S(1)} %bitcast.215, bf16[]{:T(256)} %broadcast.146), dimensions={1}, to_apply=%bitcast.148.reduce_sub_computation | reduce | bytes 2097154
  371.6 3.9 all-to-all-start
  375.5 5.0 copy.124
  380.6 23.3 %reduce.1 = bf16[4096,128]{1,0:T(8,128)(2,1)} reduce(bf16[4096,1,128]{2,1,0:T(2,128)(2,1)S(1)} %bitcast.218, bf16[]{:T(256)} %broadcast.146), dimensions={1}, to_apply=%bitcast.150.reduce_sub_computation | reduce | bytes 2097154
  406.0 4.4 all-to-all-start.3
  414.4 8.7 all-to-all-done.3
  427.5 5.6 copy.150
  433.1 7.5 copy.121
  440.6 5.2 gather_fusion
  445.9 2.7 fusion.74
  451.8 287.4 %while.19 = (s32[]{:T(128)}, bf16[16,256,128]{1,2,0:T(8,128)(2,1)}, bf16[16,256,128]{1,2,0:T(8,128)(2,1)}, f32[16,2048,128]{2,1,0:T(8,128)}, f32[16,2048,128]{2,...) while((s32[]{:T(128)}, bf16[16,256,128]{1,2,0:T(8,128)(2,1)}, ...), condition=%wide.region_5.6_spmd.clone, body=%wide.region_1.5_spmd.clone.sunk | while | flops 815987968 | bytes 27189448 | solution.py:71
  464.8 2.5 fusion.108
  482.8 2.5 fusion.108
  500.7 2.5 fusion.108
  518.6 2.5 fusion.108
  521.2 2.3 fusion.107
  536.6 2.5 fusion.108
  554.5 2.5 fusion.108
  557.1 2.4 fusion.107
  572.5 2.5 fusion.108
  590.4 2.6 fusion.108
  593.0 2.4 fusion.107
  608.4 2.6 fusion.108
  611.0 2.4 fusion.107
  626.5 2.5 fusion.108
  644.4 2.5 fusion.108
  662.4 2.5 fusion.108
  680.3 2.6 fusion.108
  682.9 2.4 fusion.107
  698.3 2.5 fusion.108
  716.2 2.5 fusion.108
  734.1 2.5 fusion.108
  739.2 9.4 bitcast_reduce_fusion
  748.6 6.6 copy.135
  755.2 9.3 bitcast_reduce_fusion.1
  764.5 4.8 copy.134
  769.3 6.2 fusion.39
  775.4 10.1 copy.136
  785.7 102.2 %reduce-scatter.3.cloned.1.call-done = f32[1,128,4,2,128]{1,4,2,3,0:T(8,128)} async-done(((f32[16,128,4,2,128]{1,4,2,3,0:T(8,128)}), f32[1,128,4,2,128]{1,4,2,3,0:T(8,128)}) %reduce-scatter.3.cloned.1.call-update) | async-done | bytes 524304 | tf_op jit(solution)/shard_map/reduce_scatter | solution.py:155
  891.1 8.8 all_gather.19
  899.9 9.5 convert_bitcast_fusion
  909.4 4.8 copy.129
  914.2 6.7 reduce.2
  922.5 3.6 all-to-all-start.4
  926.1 5.2 copy.132
  931.3 7.7 reduce.3
  939.0 2.6 reshape.134
  941.6 4.4 all-to-all-start.5
  949.6 9.8 all-to-all-done.5
  963.9 124.1 %reduce-scatter.5.cloned.1.call-done = bf16[256,2048]{0,1:T(8,128)(2,1)} async-done(((bf16[4096,2048]{0,1:T(8,128)(2,1)}), bf16[256,2048]{0,1:T(8,128)(2,1)}) %reduce-scatter.5.cloned.1.call-update) | async-done | bytes 1048592 | tf_op jit(solution)/shard_map/reduce_scatter | solution.py:171
  (525 shorter events, 209.8 us)
Async XLA Ops:
  8.0 403.2 %copy-start = (s32[1,16]{1,0:T(1,128)S(1)}, s32[1,16]{1,0:T(1,128)}, u32[]{:S(2)}) copy-start(s32[1,16]{1,0:T(1,128)} %param.19) | copy-start | bytes 196
  8.0 84.4 %all-gather.8.cloned.1.call-start = ((), (), s32[]{:S(2)}) async-start(), calls=%async_computation.9 | async-start | bytes 8912896 | tf_op jit(solution)/shard_map/all_gather | solution.py:99
  10.1 161.3 %all-gather.10.cloned.1.call-start = ((), (), s32[]{:S(2)}) async-start(), calls=%async_computation.10 | async-start | bytes 8912896 | tf_op jit(solution)/shard_map/all_gather | solution.py:100
  104.5 100.0 %all-to-all-start.1 = ((bf16[4096,2,512]{2,0,1:T(8,128)(2,1)}), bf16[4096,2,512]{2,0,1:T(8,128)(2,1)}, u32[]{:S(2)}, u32[]{:S(2)}) async-start(bf16[4096,2,512]{2,0,1:T(8,128)(2,1)} %copy.115), calls=%async_computation.1 | async-start | bytes 16777216 | tf_op jit(solution)/shard_map/all_to_all | solution.py:103
  204.5 121.6 %all-to-all-start.2 = ((bf16[4096,2,512]{2,0,1:T(8,128)(2,1)}), bf16[4096,2,512]{2,0,1:T(8,128)(2,1)}, u32[]{:S(2)}, u32[]{:S(2)}) async-start(bf16[4096,2,512]{2,0,1:T(8,128)(2,1)} %copy.118), calls=%async_computation.2 | async-start | bytes 16777216 | tf_op jit(solution)/shard_map/all_to_all | solution.py:104
  211.4 56.5 %all-gather.6.cloned.1.call-start = ((), (), s32[]{:S(2)}) async-start(), calls=%async_computation.8 | async-start | bytes 3145728 | tf_op jit(solution)/shard_map/all_gather | solution.py:106
  212.0 215.5 %all-gather.12.cloned.1.call-start = ((), (), s32[]{:S(2)}) async-start(), calls=%async_computation.13 | async-start | bytes 4456448 | tf_op jit(solution)/shard_map/all_gather | solution.py:117
  326.1 12.1 %copy-start.8 = (f32[128]{0:T(128)S(1)}, f32[128]{0:T(128)}, u32[]{:S(2)}) copy-start(f32[128]{0:T(128)} %param.14) | copy-start | bytes 1540
  326.1 12.1 %copy-start.16 = (bf16[1,128,8192]{2,1,0:T(8,128)(2,1)S(1)}, bf16[1,128,8192]{2,1,0:T(8,128)(2,1)}, u32[]{:S(2)}) copy-start(bf16[1,128,8192]{2,1,0:T(8,128)(2,1)} %all-gather.6.cloned.1.call-done) | copy-start | bytes 6291460
  371.6 34.4 %all-to-all-start = ((bf16[2,2,131072]{2,1,0:T(2,128)(2,1)}), bf16[2,2,131072]{2,1,0:T(2,128)(2,1)S(1)}, u32[]{:S(2)}, u32[]{:S(2)}) async-start(bf16[2,2,131072]{2,1,0:T(2,128)(2,1)} %reshape.128), calls=%async_computation | async-start | bytes 2097152 | tf_op jit(solution)/shard_map/all_to_all | solution.py:120
  406.0 17.1 %all-to-all-start.3 = ((bf16[2,2,131072]{2,1,0:T(2,128)(2,1)}), bf16[2,2,131072]{2,1,0:T(2,128)(2,1)}, u32[]{:S(2)}, u32[]{:S(2)}) async-start(bf16[2,2,131072]{2,1,0:T(2,128)(2,1)} %reshape.130), calls=%async_computation.3 | async-start | bytes 2097152 | tf_op jit(solution)/shard_map/all_to_all | solution.py:121
  410.4 477.5 %reduce-scatter.3.cloned.1.call-start = ((), (), s32[]{:S(2)}) async-start(), calls=%async_computation.11 | async-start | bytes 8912896 | tf_op jit(solution)/shard_map/reduce_scatter | solution.py:155
  451.8 6.9 copy-start.10
  451.8 6.9 copy-start.12
  469.7 6.9 copy-start.6
  469.8 6.9 copy-start.10
  469.8 6.9 copy-start.12
  487.7 6.9 copy-start.6
  487.7 6.9 copy-start.10
  487.7 6.9 copy-start.12
  505.6 6.9 copy-start.6
  505.6 6.9 copy-start.10
  505.6 6.9 copy-start.12
  523.6 6.9 copy-start.6
  523.6 6.9 copy-start.10
  523.6 6.9 copy-start.12
  541.5 6.9 copy-start.6
  541.5 6.9 copy-start.10
  541.5 6.9 copy-start.12
  559.5 6.9 copy-start.6
  559.5 6.9 copy-start.10
  559.5 6.9 copy-start.12
  577.4 6.9 copy-start.6
  577.4 6.9 copy-start.10
  577.4 6.9 copy-start.12
  595.4 6.9 copy-start.6
  595.4 6.9 copy-start.10
  595.4 6.9 copy-start.12
  613.5 6.9 copy-start.6
  613.5 6.9 copy-start.10
  613.5 6.9 copy-start.12
  631.4 6.9 copy-start.6
  631.4 6.9 copy-start.10
  631.4 6.9 copy-start.12
  649.3 6.9 copy-start.6
  649.3 6.9 copy-start.10
  649.4 6.9 copy-start.12
  667.3 6.9 copy-start.6
  667.3 6.9 copy-start.10
  667.3 6.9 copy-start.12
  685.3 6.9 copy-start.6
  685.3 6.9 copy-start.10
  685.3 6.9 copy-start.12
  703.2 6.9 copy-start.6
  703.2 6.9 copy-start.10
  703.2 6.9 copy-start.12
  721.1 6.9 copy-start.6
  721.1 6.9 copy-start.10
  721.2 6.9 copy-start.12
  785.6 102.3 %copy-start.9 = (f32[128]{0:T(128)S(1)}, f32[128]{0:T(128)}, u32[]{:S(2)}) copy-start(f32[128]{0:T(128)} %param.14) | copy-start | bytes 1540
  785.6 114.3 %copy-start.3 = (bf16[1,128,4096]{2,1,0:T(8,128)(2,1)S(1)}, bf16[1,128,4096]{2,1,0:T(8,128)(2,1)}, u32[]{:S(2)}) copy-start(bf16[1,128,4096]{2,1,0:T(8,128)(2,1)} %param.11) | copy-start | bytes 3145732
  785.6 302.4 %reduce-scatter.5.cloned.1.call-start = ((), (), s32[]{:S(2)}) async-start(), calls=%async_computation.12 | async-start | bytes 17825792 | tf_op jit(solution)/shard_map/reduce_scatter | solution.py:171
  922.5 19.1 %all-to-all-start.4 = ((bf16[2,2,131072]{2,1,0:T(2,128)(2,1)}), bf16[2,2,131072]{2,1,0:T(2,128)(2,1)S(1)}, u32[]{:S(2)}, u32[]{:S(2)}) async-start(bf16[2,2,131072]{2,1,0:T(2,128)(2,1)} %reshape.132), calls=%async_computation.4 | async-start | bytes 2097152 | tf_op jit(solution)/shard_map/all_to_all | solution.py:143
  941.6 17.7 %all-to-all-start.5 = ((bf16[2,2,131072]{2,1,0:T(2,128)(2,1)}), bf16[2,2,131072]{2,1,0:T(2,128)(2,1)}, u32[]{:S(2)}, u32[]{:S(2)}) async-start(bf16[2,2,131072]{2,1,0:T(2,128)(2,1)} %reshape.134), calls=%async_computation.5 | async-start | bytes 2097152 | tf_op jit(solution)/shard_map/all_to_all | solution.py:144
  (102 other events, 294.7 us)
Sparse Core Ops, SparseCore 0:
  11.6 80.7 all-gather.7
  95.1 76.2 all-gather.9
  344.9 50.6 all-gather.11
  785.7 102.1 reduce-scatter.2
  909.5 178.4 reduce-scatter.4
Sparse Core Ops, SparseCore 1:
  213.4 54.4 all-gather.5
where the time goes:
time: 1120 us; the launch traced here: 1100 us
  waiting for transfers between devices  502 us (45%)
  matrix products  209 us (19%)
  local copies, waits for them, and re-layouts  167 us (15%)
  other arithmetic  103 us (9%)
  loops' own time  62.3 us (6%)
  starting transfers between devices  30.6 us (3%)
  between operations  16.7 us (1%)
    reduce_scatter x1, waiting for transfers between devices, shards(): lax.psum_scatter(lax.dot_general(picture_rows, joined, (((0,), (0,)), (()...  124 us
    reduce_scatter x1, waiting for transfers between devices, shards(): lax.psum_scatter(image_gradients, 'dp', scatter_dimension=0, tiled=True)  102 us
    all_gather x1, waiting for transfers between devices, shards(): lax.all_gather(key_projection_weight, 'dp', axis=0, tiled=True)  80.2 us
    another operation x1, loops' own time, document_pass(): lax.map(per_head, jnp.arange(query_heads, dtype=jnp.int32))  62.3 us
    unnamed x4, other arithmetic  60 us
    all_gather x1, waiting for transfers between devices, shards(): lax.all_gather(value_projection_weight, 'dp', axis=0, tiled=True)  60 us
    all_to_all x1, waiting for transfers between devices, shards(): lax.all_to_all(block_value, 'sp', split_axis=1, concat_axis=0, tiled=True)  51.8 us
    all_gather x1, waiting for transfers between devices, shards(): lax.all_gather(vision, 'sp', axis=2, tiled=True).reshape(row_sum_total, -1)  43.9 us
  transfers between devices with their start and end apart: 12, of which 9 were waited for; matrix products, arithmetic and copies ran while one was open for 13% of the time, Pallas kernels for 0%

commit v1 on v0

v1 whole, which is shorter than its diff:
```python
import functools
import math

import jax
import jax.numpy as jnp
from jax import lax
from jax.experimental import pallas as pl
from jax.experimental.pallas import tpu as pltpu
from jax.sharding import PartitionSpec as P

KEY_VALUE_HEADS = 8
HEAD_SIZE = 128
TILE = 128

norm_epsilon = 1e-05
bf16 = jnp.bfloat16
f32 = jnp.float32
f16 = jnp.float16
SUM_SCALE = 16.0


def key_norm(key_before_projection, key_gain):
    mean_square = jnp.mean(key_before_projection * key_before_projection, axis=-1, keepdims=True)
    return key_before_projection * lax.rsqrt(mean_square + norm_epsilon) * key_gain


def after(a, *done):
    return lax.optimization_barrier((a, *done))[0]


def swap_core(a):
    n = lax.axis_size("dp")
    return lax.ppermute(a, "dp", [(i, i ^ 1) for i in range(n)])


def swap_x(a):
    n = lax.axis_size("dp")
    return lax.ppermute(a, "dp", [(i, i ^ 2) for i in range(n)])


def shift_chip(a, k, r=0):
    n = lax.axis_size("dp")
    return lax.ppermute(a, "dp", [(i, ((i + 4 * k) % n) ^ (2 * r)) for i in range(n)])


def swap_y(a):
    return lax.ppermute(a, "sp", [(0, 1), (1, 0)])


def gather_y(a):
    if lax.axis_size("sp") == 2:
        return [a, swap_y(a)]
    whole = lax.all_gather(a, "sp", axis=0, tiled=False)
    return [whole[i] for i in range(lax.axis_size("sp"))]


def exchange_y(blocks):
    if lax.axis_size("sp") == 2:
        return [blocks[0], swap_y(blocks[1])]
    got = lax.all_to_all(jnp.stack(blocks), "sp", split_axis=0, concat_axis=0, tiled=True)
    return [got[i] for i in range(lax.axis_size("sp"))]


def split_y(a, axis):
    size = lax.axis_size("sp")
    parts = jnp.split(a, size, axis=axis)
    if size == 2:
        s = lax.axis_index("sp")
        half = a.shape[axis] // 2
        return [lax.dynamic_slice_in_dim(a, (s ^ r) * half, half, axis) for r in range(2)]
    return parts


def join_y(parts, axis):
    if lax.axis_size("sp") == 2:
        s = lax.axis_index("sp")
        return jnp.where(
            s == 0,
            jnp.concatenate(parts, axis=axis),
            jnp.concatenate(parts[::-1], axis=axis),
        )
    return jnp.concatenate(parts, axis=axis)


def turns(total):
    return [*range(2, total), 1, 0]


def reduce_chips(keep, send, total, kind=bf16):
    low = []
    for j in turns(total):
        other = swap_x(send[j])
        if j == 0:
            return [keep[0]], [*low, other]
        low.append(shift_chip((keep[j] + other.astype(f32)).astype(kind), -j))


def gather_chips(block, total):
    column = [None] * total
    column[0] = block
    up, down = block, block
    for step in range(1, total // 2 + 1):
        up = shift_chip(up, 1)
        column[step] = up
        if step < total - step:
            down = shift_chip(down, -1)
            column[total - step] = down
    return [b for block in column for b in (block, swap_x(block))]


def attention_kernel(group, scale, chunk, blocks, parts, images, pos_ref, start_ref, base_ref, *refs):
    q_ref, g_ref = refs[:2]
    kv_refs = refs[2 : 2 + blocks]
    att_ref, dq_ref = refs[2 + blocks : 4 + blocks]
    grad_refs = refs[4 + blocks : -12]
    qs, gs, gt, kv, kc, vc, kct, vct, weights, tops, turned, acc = refs[-12:]
    size = HEAD_SIZE
    slots = start_ref.shape[1]
    tokens = kv.shape[0] // images
    span = chunk * tokens
    doc = pl.program_id(1)
    rows = group * TILE

    @pl.when(doc == 0)
    def _():
        acc[...] = jnp.zeros_like(acc)
        for part in range(parts):

            @pl.when(pl.program_id(0) * parts // pl.num_programs(0) == part)
            def _():
                at = 0
                for ref in kv_refs[part::parts]:
                    kv[at : at + ref.shape[0], :] = ref[...]
                    at += ref.shape[0]

    for i in range(slots):
        row = pl.ds(pl.multiple_of(pos_ref[doc, i] * tokens, tokens), tokens)
        here = slice(i * tokens, (i + 1) * tokens)
        inside = slice(i % chunk * tokens, (i % chunk + 1) * tokens)
        k, v = kv[row, :size], kv[row, size:]
        kc[here, :] = k
        vc[here, :] = v
        kct[i // chunk, :, inside] = k.T
        vct[i // chunk, :, inside] = v.T

    def acc_rows(i):
        return pl.ds(pl.multiple_of(pos_ref[doc, i] * tokens, tokens), tokens)

    def tile_step(tile, carry):
        base = base_ref[tile]
        here = pl.ds(pl.multiple_of(tile * TILE, TILE), TILE)
        for h in range(group):
            qs[h * TILE : (h + 1) * TILE, :] = q_ref[here, h * size : (h + 1) * size]
            gs[h * TILE : (h + 1) * TILE, :] = g_ref[here, h * size : (h + 1) * size]
        gt[...] = gs[...].T
        n = jnp.int32(0)
        for i in range(slots):
            n = n + (start_ref[doc, i] < base + TILE).astype(jnp.int32)
        position = base + lax.broadcasted_iota(jnp.int32, (1, rows), 1) % TILE

        def run(chunks):
            top = jnp.full((1, rows), -1e30, f32)
            total = jnp.zeros((1, rows), f32)
            for j in range(chunks):
                s = lax.dot_general(
                    kc[j * span : (j + 1) * span, :],
                    qs[...],
                    (((1,), (1,)), ((), ())),
                    preferred_element_type=f32,
                )
                parts = []
                for i in range(chunk):
                    hidden = jnp.where(position >= start_ref[doc, chunk * j + i], 0.0, -1e30)
                    part = s[i * tokens : (i + 1) * tokens] * (scale * math.log2(math.e))
                    parts.append(part + hidden)
                s = jnp.concatenate(parts, 0)
                now = jnp.maximum(top, jnp.max(s, axis=0, keepdims=True))
                e = jnp.exp2(s - now)
                weights[j] = e
                tops[j] = now
                total = total * jnp.exp2(top - now) + jnp.sum(e, axis=0, keepdims=True)
                top = now
            inverse = 1.0 / total
            turned[...] = jnp.zeros_like(turned)
            for j in range(chunks):
                low = (weights[j] * (jnp.exp2(tops[j] - top) * inverse)).astype(bf16)
                turned[...] += jnp.dot(vct[j], low, preferred_element_type=f32)
                dv = jnp.dot(low, gs[...], preferred_element_type=f32)
                for i in range(chunk):
                    acc[acc_rows(chunk * j + i), size:] += dv[i * tokens : (i + 1) * tokens]
            att = turned[...].astype(bf16)
            for h in range(group):
                att_ref[here, h * size : (h + 1) * size] = att[:, h * TILE : (h + 1) * TILE].T
            delta = jnp.sum(gt[...].astype(f32) * att.astype(f32), axis=0, keepdims=True)
            turned[...] = jnp.zeros_like(turned)
            for j in range(chunks):
                dp = lax.dot_general(
                    vc[j * span : (j + 1) * span, :],
                    gs[...],
                    (((1,), (1,)), ((), ())),
                    preferred_element_type=f32,
                )
                p = weights[j] * (jnp.exp2(tops[j] - top) * (inverse * scale))
                ds = (p * (dp - delta)).astype(bf16)
                turned[...] += jnp.dot(kct[j], ds, preferred_element_type=f32)
                dk = jnp.dot(ds, qs[...], preferred_element_type=f32)
                for i in range(chunk):
                    acc[acc_rows(chunk * j + i), :size] += dk[i * tokens : (i + 1) * tokens]
            dq = turned[...].astype(bf16)
            for h in range(group):
                dq_ref[here, h * size : (h + 1) * size] = dq[:, h * TILE : (h + 1) * TILE].T

        used = (n + chunk - 1) // chunk
        for chunks in range(1, slots // chunk + 1):
            pl.when(used == chunks)(functools.partial(run, chunks))
        return carry

    lax.fori_loop(0, q_ref.shape[0] // TILE, tile_step, 0)

    @pl.when(doc == pl.num_programs(1) - 1)
    def _():
        at = 0
        for ref in grad_refs:
            ref[...] = acc[at : at + ref.shape[0], :].astype(ref.dtype)
            at += ref.shape[0]


def attention(both, kv_blocks, parts, pos, starts, bases):
    docs, slots = starts.shape
    length = both.shape[0] // docs
    kv_rows = sum(b.shape[0] for b in kv_blocks[::parts])
    kv_cols = kv_blocks[0].shape[1] * parts
    heads = kv_cols // (2 * HEAD_SIZE)
    width = both.shape[1] // 2
    span = width // heads
    group = span // HEAD_SIZE
    images = lax.axis_size("dp")
    tokens = kv_rows // images
    chunk = next(c for c in (4, 2, 1) if slots % c == 0)
    rows = group * TILE
    q_spec = pl.BlockSpec((length, span), lambda h, d, *_: (d, h))
    g_spec = pl.BlockSpec((length, span), lambda h, d, *_: (d, heads + h))
    each = heads // parts
    kv_specs = [
        pl.BlockSpec(
            (b.shape[0], 2 * HEAD_SIZE),
            lambda h, d, *_, part=i % parts: (0, jnp.clip(h - part * each, 0, each - 1)),
        )
        for i, b in enumerate(kv_blocks)
    ]
    count = lax.axis_size("dp") // 2
    grad_rows = kv_rows // count
    grad_spec = pl.BlockSpec((grad_rows, 2 * HEAD_SIZE), lambda h, d, *_: (0, h))
    grad_shapes = [
        jax.ShapeDtypeStruct((grad_rows, kv_cols), f32 if i < count // 2 else bf16)
        for i in range(count)
    ]
    grid_spec = pltpu.PrefetchScalarGridSpec(
        num_scalar_prefetch=3,
        grid=(heads, docs),
        in_specs=[q_spec, g_spec, *kv_specs],
        out_specs=[q_spec, q_spec] + [grad_spec] * count,
        scratch_shapes=[
            pltpu.VMEM((rows, HEAD_SIZE), bf16),
            pltpu.VMEM((rows, HEAD_SIZE), bf16),
            pltpu.VMEM((HEAD_SIZE, rows), bf16),
            pltpu.VMEM((kv_rows, 2 * HEAD_SIZE), bf16),
            pltpu.VMEM((slots * tokens, HEAD_SIZE), bf16),
            pltpu.VMEM((slots * tokens, HEAD_SIZE), bf16),
            pltpu.VMEM((slots // chunk, HEAD_SIZE, chunk * tokens), bf16),
            pltpu.VMEM((slots // chunk, HEAD_SIZE, chunk * tokens), bf16),
            pltpu.VMEM((slots // chunk, chunk * tokens, rows), f32),
            pltpu.VMEM((slots // chunk, 1, rows), f32),
            pltpu.VMEM((HEAD_SIZE, rows), f32),
            pltpu.VMEM((kv_rows, 2 * HEAD_SIZE), f32),
        ],
    )
    out_shape = jax.ShapeDtypeStruct((docs * length, width), bf16)
    return pl.pallas_call(
        functools.partial(
            attention_kernel, group, 1.0 / math.sqrt(HEAD_SIZE), chunk, len(kv_blocks), parts, images
        ),
        grid_spec=grid_spec,
        out_shape=[out_shape, out_shape, *grad_shapes],
        compiler_params=pltpu.CompilerParams(
            vmem_limit_bytes=(12 << 20) + 16 * kv_rows * 2 * HEAD_SIZE + 24 * length * span
        ),
        cost_estimate=pl.CostEstimate(
            flops=12 * docs * length * width * slots * tokens,
            bytes_accessed=8 * docs * length * width + 5 * kv_rows * kv_cols,
            transcendentals=docs * length * width // HEAD_SIZE * slots * tokens,
        ),
        name="attention",
    )(pos, starts, bases, both, both, *kv_blocks)


def whole_call(kernel, out_shape, args, flops, name, scalar=None):
    vmem = pl.BlockSpec(memory_space=pltpu.VMEM)
    smem = pl.BlockSpec(memory_space=pltpu.SMEM)
    scalars = [] if scalar is None else [scalar.reshape(-1).astype(jnp.int32)]
    moved = sum(a.size * a.dtype.itemsize for a in (*args, *out_shape))
    return pl.pallas_call(
        kernel,
        out_shape=out_shape,
        in_specs=[smem] * len(scalars) + [vmem] * len(args),
        out_specs=[vmem] * len(out_shape),
        compiler_params=pltpu.CompilerParams(vmem_limit_bytes=16 * 1024 * 1024),
        cost_estimate=pl.CostEstimate(flops=flops, bytes_accessed=moved, transcendentals=0),
        name=name,
    )(*scalars, *args)


def in_order(core, own, other):
    return jnp.where(core == 0, own, other), jnp.where(core == 0, other, own)


def project(seen, weights, core):
    count = len(weights)
    tokens, features = seen[0][0].shape
    width = weights[0][0].shape[1] // 2

    def kernel(core_ref, *refs):
        outs = refs[4 * count :]
        totals = [None, None]
        for y in range(count):
            own, other = refs[2 * count + 2 * y : 2 * count + 2 * y + 2]
            w = jnp.concatenate(in_order(core_ref[0], own[...], other[...]), 0)
            for r in range(2):
                term = jnp.dot(refs[r * count + y][...], w, preferred_element_type=f32)
                totals[r] = term if totals[r] is None else totals[r] + term
        for total, out in zip(totals, outs, strict=True):
            for h in range(width // HEAD_SIZE):
                for kind in range(2):
                    c = (2 * h + kind) * HEAD_SIZE
                    t = total[:, kind * width + h * HEAD_SIZE :][:, :HEAD_SIZE]
                    out[:, c : c + HEAD_SIZE] = (t * SUM_SCALE).astype(out.dtype)

    shape = (tokens, 2 * width)
    shapes = [jax.ShapeDtypeStruct(shape, f32), jax.ShapeDtypeStruct(shape, f32)]
    flops = 8 * tokens * width * features * count
    args = [*seen[0], *seen[1], *(w for pair in weights for w in pair)]
    return whole_call(kernel, shapes, args, flops, "project", core)


def total_of(refs):
    total = refs[0][...]
    for ref in refs[1:]:
        total = total + ref[...].astype(f32)
    return total


def norm_forward(high, low, gain, core, halves):
    terms = [*high, *low]

    def kernel(core_ref, *refs):
        gain_ref, pre_ref = refs[len(terms) : len(terms) + 2]
        outs = refs[len(terms) + 2 :]
        total = total_of(refs[: len(terms)]) * (1.0 / SUM_SCALE)
        pre_ref[...] = total
        blocks = []
        for c in range(0, total.shape[1], 2 * HEAD_SIZE):
            blocks.append(key_norm(total[:, c : c + HEAD_SIZE], gain_ref[...]).astype(bf16))
            blocks.append(total[:, c + HEAD_SIZE : c + 2 * HEAD_SIZE].astype(bf16))
        low = jnp.concatenate(blocks, 1)
        if halves == 2:
            half = low.shape[1] // 2
            outs[0][...], outs[1][...] = in_order(core_ref[0], low[:, :half], low[:, half:])
        else:
            outs[0][...] = low

    rows, cols = terms[0].shape
    shapes = [jax.ShapeDtypeStruct((rows, cols), f32)]
    shapes += [jax.ShapeDtypeStruct((rows, cols // halves), bf16)] * halves
    outs = whole_call(kernel, shapes, [*terms, gain], 8 * rows * cols, "norm_forward", core)
    return outs[0], outs[1:]


def sum_terms(parts):
    counts = [len(high) + len(low) for high, low in parts]
    terms = [t for high, low in parts for t in (*high, *low)]

    def kernel(*refs):
        mine_ref, theirs_ref = refs[len(terms) :]
        half, cols = mine_ref.shape[0], refs[0].shape[1]
        for p, count in enumerate(counts):
            total = total_of(refs[sum(counts[:p]) : sum(counts[:p]) + count])
            here = slice(p * cols, (p + 1) * cols)
            mine_ref[:, here] = total[:half]
            theirs_ref[:, here] = total[half:]

    rows, cols = terms[0].shape
    shapes = [jax.ShapeDtypeStruct((rows // 2, len(parts) * cols), f32)] * 2
    return whole_call(kernel, shapes, terms, rows * cols * len(terms), "sum_terms")


def norm_backward(parts, high, low, pre, gain, core):
    terms = [*parts, *high, *low]

    def kernel(core_ref, *refs):
        pre_ref, gain_ref, out_ref = refs[len(terms) :]
        if parts:
            total = jnp.concatenate(in_order(core_ref[0], refs[0][...], refs[1][...]), 1)
        else:
            total = total_of(refs[: len(terms)])
        for c in range(0, total.shape[1], 2 * HEAD_SIZE):
            k = slice(c, c + HEAD_SIZE)
            x = pre_ref[:, k]
            inverse = lax.rsqrt(jnp.mean(x * x, axis=-1, keepdims=True) + norm_epsilon)
            up = total[:, k] * gain_ref[...]
            mean = jnp.mean(up * x, axis=-1, keepdims=True)
            out_ref[:, k] = (inverse * (up - x * (inverse * inverse * mean))).astype(bf16)
            v = slice(c + HEAD_SIZE, c + 2 * HEAD_SIZE)
            out_ref[:, v] = total[:, v].astype(bf16)

    shapes = [jax.ShapeDtypeStruct(pre.shape, bf16)]
    args = [*terms, pre, gain]
    return whole_call(kernel, shapes, args, 12 * pre.size, "norm_backward", core)[0]


def place_columns(pieces, width, places):
    arrays = list({id(a): a for a, _, _ in pieces}.values())
    index = {id(a): i for i, a in enumerate(arrays)}
    rows = min(a.shape[0] for a in arrays)

    def kernel(place_ref, *refs):
        for i, (a, row, col) in enumerate(pieces):
            to = pl.ds(pl.multiple_of(place_ref[i] * width, width), width)
            refs[-1][:, to] = refs[index[id(a)]][row : row + rows, col : col + width]

    shapes = [jax.ShapeDtypeStruct((rows, len(pieces) * width), arrays[0].dtype)]
    return whole_call(kernel, shapes, arrays, 0, "place_columns", places)[0]


def weight_gradient(seen, back, core):
    count, parts = len(seen), len(back)

    def kernel(core_ref, *refs):
        mine_ref, theirs_ref = refs[-2:]
        half, cols = mine_ref.shape[0], refs[count].shape[1]
        for p in range(parts):
            total = None
            for a, b in zip(refs[:count], refs[count * (p + 1) : count * (p + 2)], strict=True):
                term = lax.dot_general(
                    a[...], b[...], (((0,), (0,)), ((), ())), preferred_element_type=f32
                )
                total = term if total is None else total + term
            here = slice(p * cols, (p + 1) * cols)
            mine, theirs = in_order(core_ref[0], total[:half], total[half:])
            mine_ref[:, here] = mine
            theirs_ref[:, here] = theirs

    half, cols = seen[0].shape[1] // 2, back[0][0].shape[1] * parts
    shapes = [jax.ShapeDtypeStruct((half, cols), f32)] * 2
    flops = 4 * half * cols * count * seen[0].shape[0]
    args = [*seen, *(b for part in back for b in part)]
    return whole_call(kernel, shapes, args, flops, "weight_gradient", core)


def split_heads(parts, index):
    ys = len(parts[0])
    rows, cols = parts[0][0][0].shape
    args = [t for part in parts for block in part for t in block]

    def kernel(index_ref, *refs):
        outs = refs[-2:]

        def place(order):
            it = iter(refs)
            for p, part in enumerate(parts):
                for block, to in zip(part, order, strict=True):
                    terms = [next(it)[...].astype(f32) for _ in block]
                    total = sum(terms[1:], terms[0])
                    for c in range(0, cols, HEAD_SIZE):
                        h = (to * len(parts) + p) * (cols // 2)
                        h += c // (2 * HEAD_SIZE) * HEAD_SIZE
                        out = outs[c // HEAD_SIZE % 2]
                        out[:, h : h + HEAD_SIZE] = total[:, c : c + HEAD_SIZE]

        if ys == 2:
            for i in range(2):
                pl.when(index_ref[0] == i)(functools.partial(place, (i, 1 - i)))
        else:
            place(range(ys))

    shapes = [jax.ShapeDtypeStruct((rows, ys * len(parts) * cols // 2), f32)] * 2
    return whole_call(kernel, shapes, args, 0, "split_heads", index)


def shards(
    vision,
    key_projection_weight,
    value_projection_weight,
    key_gain,
    queries,
    out_grad,
    image_ids,
    image_counts,
    image_starts,
):
    dp = lax.axis_size("dp")
    sp = lax.axis_size("sp")
    levels = dp // 4
    d = lax.axis_index("dp")
    s = lax.axis_index("sp")
    z, x, core = d // 4, (d // 2) % 2, d % 2
    tokens = vision.shape[0] * vision.shape[1]
    own_vision = vision.reshape(tokens, vision.shape[2])
    heads = KEY_VALUE_HEADS // sp
    rows_here = key_projection_weight.shape[0]

    keys = split_y(key_projection_weight, 1)
    values = split_y(value_projection_weight, 1)
    weights = exchange_y(
        [jnp.concatenate(pair, 1) for pair in zip(keys, values, strict=True)]
    )
    weights = [(w, swap_core(w)) for w in weights]

    order = [*range(1, levels), 0]
    pieces = {}
    for j in order:
        for r in range(2):
            chip = (z + j) % levels * 2 + (x ^ r)
            piece = lax.dynamic_slice_in_dim(own_vision, chip * 2 * rows_here, 2 * rows_here, 1)
            if j > 1:
                piece = after(piece, pieces[j - 1, r])
            pieces[j, r] = piece if j == 0 and r == 0 else shift_chip(piece, j, r)
    seen = [None] * (2 * levels)
    moved = [weights[-1][0]]
    terms = [None] * levels
    for n, j in enumerate(order):
        for r in range(2):
            piece = pieces[j, r]
            if len(moved) > 1:
                piece = after(piece, moved[-2])
            seen[2 * j + r] = gather_y(piece)
            moved.append(seen[2 * j + r][-1])
        terms[j] = project(seen[2 * j : 2 * j + 2], weights, core)

    halves = 2 if heads % 2 == 0 else 1
    queries, out_grad = after(queries, moved[-1]), after(out_grad, moved[-1])
    queries, out_grad = split_y(queries[0], 1), split_y(out_grad[0], 1)
    both = exchange_y([jnp.concatenate(pair, 1) for pair in zip(queries, out_grad, strict=True)])
    both = jnp.concatenate(both, 0)
    length = both.shape[0]
    if halves == 2:
        half = both.shape[1] // 4
        cuts = [
            jnp.concatenate(
                [
                    lax.dynamic_slice_in_dim(both, (2 * kind + (core ^ c)) * half, half, 1)
                    for kind in range(2)
                ],
                1,
            )
            for c in range(2)
        ]
        both = jnp.concatenate((cuts[0], swap_core(cuts[1])), 0)

    gain = key_gain.reshape(1, HEAD_SIZE)
    high, low = reduce_chips([t[0] for t in terms], [t[1].astype(f16) for t in terms], levels, f16)
    total = sum([a.astype(f32) for a in low], high[0])
    pre, pairs = norm_forward([total], [], gain, core, halves)
    block = pairs[0]
    if halves == 2:
        block = jnp.concatenate((block, swap_core(pairs[1])), 0)
    if halves == 2:
        column = gather_chips(block, levels)
        kv_blocks = column[::2] + column[1::2]
    else:
        column = gather_chips(block, levels)
        kv_blocks = [*column, swap_core(jnp.concatenate(column, 0))]

    ids = image_ids[0].astype(jnp.int32)
    slot = jnp.arange(ids.shape[0], dtype=jnp.int32)
    first = jnp.where(slot == 0, -1, image_starts[0])
    first = jnp.where(slot < image_counts[0], first, 1 << 30)
    before = (first[None, :] < first[:, None]) | (
        (first[None, :] == first[:, None]) & (slot[None, :] < slot[:, None])
    )
    rank = jnp.sum(before.astype(jnp.int32), axis=1)
    turn = (rank[None, :] == slot[:, None]).astype(jnp.int32)
    table = jnp.sum(turn[None] * jnp.stack((ids, first))[:, None, :], axis=2)[None]
    if halves == 2:
        table = jnp.concatenate((table, swap_core(table)), 0)
    ids, first = table[:, 0], table[:, 1]
    level, far, mate = (z - ids // 4) % levels, x ^ (ids // 2 % 2), core ^ (ids % 2)
    if halves == 2:
        place = (far * levels + level) * 2 + mate
    else:
        place = (mate * levels + level) * 2 + far
    local = length // sp
    at = jnp.arange(length // TILE, dtype=jnp.int32) * TILE
    if sp == 2:
        at = (at + s * local) % length
    attended, grad_query, *blocks = attention(both, kv_blocks, 1, place, first, at)

    width = attended.shape[1]
    sources = [(attended, 0), (grad_query, 0)]
    if halves == 2:
        theirs = swap_core(jnp.concatenate((attended[length:], grad_query[length:]), 1))
        sources += [(theirs, 0), (theirs, width)]
    got = exchange_y(
        [
            jnp.concatenate(
                [a[y * local : (y + 1) * local, c : c + width] for a, c in sources], 1
            )
            for y in range(sp)
        ]
    )
    pieces = [[], []]
    for y in range(sp):
        for i, (a, c) in enumerate(sources):
            own = y == 0 and sp == 2
            pieces[i % 2].append((a, 0, c) if own else (got[y], 0, i * width))
    ys = [s ^ y if sp == 2 else y for y in range(sp)]
    places = jnp.stack([y * halves + (core ^ c) * (halves - 1) for y in ys for c in range(halves)])
    attended_out, query_out = [place_columns(p, width, places) for p in pieces]

    keeps, sends = blocks[:levels], blocks[levels:]
    if halves == 1:
        sums = [k + swap_core(a).astype(f32) for k, a in zip(keeps, sends, strict=True)]
        keeps = [a[:tokens] for a in sums]
        sends = [a[tokens:].astype(bf16) for a in sums]
        high, low = reduce_chips(keeps, sends, levels)
        back = norm_backward([], high, low, pre, gain, core)
    else:
        totals = [reduce_chips(keeps, sends, levels)]
        mine, theirs = sum_terms(totals)
        back = norm_backward((mine, swap_core(theirs)), [], [], pre, gain, core)
    back = after(back, *got)
    back = [gather_chips(b, levels) for b in jnp.split(back, halves, axis=1)]

    for p in range(len(back) - 1):
        back[p][0] = after(back[p][0], back[p + 1][1], *back[p + 1][2::2])
    grads = []
    for part in back:
        if grads:
            part = [after(part[0], *(a for y in grads[-1] for a in y)), *part[1:]]
        sent = []
        for y in reversed(range(sp)):
            mine, theirs = weight_gradient([block[y] for block in seen], [part], core)
            other = swap_core(theirs)
            if y > 0 or sp > 2:
                sent.append((mine + other).astype(bf16))
        if sp == 2:
            grads.append([(mine, other), (swap_y(sent[0]),)])
        else:
            grads.append([(a,) for a in exchange_y(sent[::-1])])
    grad_key, grad_value = split_heads(grads, s)
    return attended_out[None], query_out[None], grad_key, grad_value


def solution(mesh):
    return jax.shard_map(
        shards,
        mesh=mesh,
        in_specs=(
            P("dp", None, "sp"),
            P(("sp", "dp"), None),
            P(("sp", "dp"), None),
            P(),
            P("dp", "sp", None),
            P("dp", "sp", None),
            P("dp", None),
            P("dp"),
            P("dp", None),
        ),
        out_specs=(
            P("dp", "sp", None),
            P("dp", "sp", None),
            P(("sp", "dp"), None),
            P(("sp", "dp"), None),
        ),
        check_vma=False,
    )
```

time: 1120 us -> 245 us (0.22); the launches traced: 1100 us -> 247 us
  waiting for transfers between devices: 502 us -> 113 us
  matrix products: 209 us -> 0 us
  local copies, waits for them, and re-layouts: 167 us -> 7.05 us
  other arithmetic: 103 us -> 8.54 us
  loops' own time: 62.3 us -> 0 us
  starting transfers between devices: 30.6 us -> 76.8 us
  Pallas kernels: 0 us -> 39.6 us
  between operations: 16.7 us -> 2.2 us
    reduce_scatter x2 -> x0, waiting for transfers between devices: 226 us -> none  [the longest x1 124 us: shards(): lax.psum_scatter(lax.dot_general(picture_rows, joined, (((0,), (0,)), (()...]
    dot_general x100 -> x0, matrix products: 209 us -> none  [the longest x16 40.5 us: head_pass(): jnp.dot(probs_low.T, grad_head, preferred_element_type=jnp.float32)]
    all_gather x4 -> x0, waiting for transfers between devices: 184 us -> none  [the longest x1 80.2 us: shards(): lax.all_gather(key_projection_weight, 'dp', axis=0, tiled=True)]
    ppermute x0 -> x66, waiting for transfers between devices: none -> 113 us  [the longest x22 51.9 us: shift_chip(): lax.ppermute(a, 'dp', [(i, (i + 4 * k) % n ^ 2 * r) for i in range(n)])]
    all_to_all x6 -> x0, waiting for transfers between devices: 91.3 us -> none  [the longest x1 51.8 us: shards(): lax.all_to_all(block_value, 'sp', split_axis=1, concat_axis=0, tiled=True)]
    ppermute x0 -> x66, starting transfers between devices: none -> 76.8 us  [the longest x20 36.1 us: swap_x(): return lax.ppermute(a, 'dp', [(i, i ^ 2) for i in range(n)])]
    another operation x1 -> x0, loops' own time: 62.3 us -> none  [document_pass(): lax.map(per_head, jnp.arange(query_heads, dtype=jnp.int32))]
    unnamed x4 -> x0, other arithmetic: 60 us -> none
  transfers between devices with their start and end apart: 12 -> 66, of which waited for: 9 -> 34; matrix products, arithmetic and copies ran while one was open for 13% -> 4% of each run, Pallas kernels for 0% -> 4%
where the time goes in v1:
time: 245 us; the launch traced here: 247 us
  waiting for transfers between devices  113 us (46%)
  starting transfers between devices  76.8 us (31%)
  Pallas kernels  39.6 us (16%)
  other arithmetic  8.54 us (3%)
  local copies, waits for them, and re-layouts  7.05 us (3%)
    ppermute x22, waiting for transfers between devices, shift_chip(): lax.ppermute(a, 'dp', [(i, (i + 4 * k) % n ^ 2 * r) for i in range(n)])  51.9 us
    ppermute x20, waiting for transfers between devices, swap_x(): return lax.ppermute(a, 'dp', [(i, i ^ 2) for i in range(n)])  43 us
    ppermute x20, starting transfers between devices, swap_x(): return lax.ppermute(a, 'dp', [(i, i ^ 2) for i in range(n)])  36.1 us
    ppermute x22, starting transfers between devices, shift_chip(): lax.ppermute(a, 'dp', [(i, (i + 4 * k) % n ^ 2 * r) for i in range(n)])  25.2 us
    pallas_call x1, Pallas kernels, attention(): pl.pallas_call(functools.partial(attention_kernel, group, 1.0 / math.sqrt...  24.2 us
    ppermute x13, waiting for transfers between devices, swap_y(): return lax.ppermute(a, 'sp', [(0, 1), (1, 0)])  16.6 us
    pallas_call x14, Pallas kernels, whole_call(): pl.pallas_call(kernel, out_shape=out_shape, in_specs=[smem] * len(scalars...  15.4 us
    ppermute x13, starting transfers between devices, swap_y(): return lax.ppermute(a, 'sp', [(0, 1), (1, 0)])  12.6 us
  transfers between devices with their start and end apart: 66, of which 34 were waited for; matrix products, arithmetic and copies ran while one was open for 4% of the time, Pallas kernels for 4%

profile of v1, /device:TPU:0, one launch (start us, length us, event | category | flops | bytes accessed | tf_op | source)
XLA Modules:
  0.0 247.1 jit_solution(13521617193600978115)
XLA Ops:
  2.1 3.0 %collective-permute-start.5 = (bf16[256,1024]{1,0:T(8,128)(2,1)S(1)}, bf16[256,1024]{1,0:T(8,128)(2,1)S(1)}, u32[]{:S(2)}, u32[]{:S(2)}) collective-permute-start(bf16[256,1024]{1,0:T(8,128)(2,1)S(1)} %pad_maximum_fusion.6), channel_id=1, source_target_pairs={{0,1},{1,0},{2,3},{3,2},{4,5},{5,4},{6,7},{7,6},{8,9},{9,8},{10,11... | collective-permute-start | bytes 1572872 | tf_op jit(solution)/shard_map/ppermute | solution.py:47
  5.9 1.6 collective-permute-start.12
  7.5 2.5 %collective-permute-start.2 = (bf16[128,512]{1,0:T(8,128)(2,1)S(1)}, bf16[128,512]{1,0:T(8,128)(2,1)S(1)}, u32[]{:S(2)}, u32[]{:S(2)}) collective-permute-start(bf16[128,512]{1,0:T(8,128)(2,1)S(1)} %get-tuple-element.109), channel_id=1, source_target_pairs={{0,12},{2,14},{4,8},{6,10},{8,20},{10,22},{12,16},{14,18},{16,28},... | collective-permute-start | bytes 393224 | tf_op jit(solution)/shard_map/ppermute | solution.py:43
  10.0 3.4 %collective-permute-done.12.refs_0_.refs_2_ = bf16[128,512]{1,0:T(8,128)(2,1)S(1)} collective-permute-done((bf16[128,512]{1,0:T(8,128)(2,1)S(1)}, bf16[128,512]{1,0:T(8,128)(2,1)S(1)}, u32[]{:S(2)}, u32[]{:S(2)}) %collective-permute-start.12) | collective-permute-done | bytes 131104 | tf_op jit(solution)/shard_map/ppermute | solution.py:43
  14.1 3.9 %collective-permute-done.2.refs_2_.refs_3_ = bf16[128,512]{1,0:T(8,128)(2,1)S(1)} collective-permute-done((bf16[128,512]{1,0:T(8,128)(2,1)S(1)}, bf16[128,512]{1,0:T(8,128)(2,1)S(1)}, u32[]{:S(2)}, u32[]{:S(2)}) %collective-permute-start.2) | collective-permute-done | bytes 131104 | tf_op jit(solution)/shard_map/ppermute | solution.py:43
  19.6 1.5 collective-permute-start.15
  21.1 3.4 %collective-permute-done.13.refs_0_.refs_4_ = bf16[128,512]{1,0:T(8,128)(2,1)S(1)} collective-permute-done((bf16[128,512]{1,0:T(8,128)(2,1)S(1)}, bf16[128,512]{1,0:T(8,128)(2,1)S(1)}, u32[]{:S(2)}, u32[]{:S(2)}) %collective-permute-start.13) | collective-permute-done | bytes 131104 | tf_op jit(solution)/shard_map/ppermute | solution.py:43
  24.5 2.1 collective-permute-start.14
  26.7 1.6 collective-permute-done.3.refs_2_.refs_5_
  31.1 3.2 %collective-permute-done.4.refs_2_.refs_7_ = bf16[128,512]{1,0:T(8,128)(2,1)S(1)} collective-permute-done((bf16[128,512]{1,0:T(8,128)(2,1)}, bf16[128,512]{1,0:T(8,128)(2,1)S(1)}, u32[]{:S(2)}, u32[]{:S(2)}) %collective-permute-start.4) | collective-permute-done | bytes 131104 | tf_op jit(solution)/shard_map/ppermute | solution.py:43
  35.4 1.5 collective-permute-start.8
  36.9 3.9 %collective-permute-done.16.refs_1_.refs_4_ = bf16[128,512]{1,0:T(8,128)(2,1)S(1)} collective-permute-done((bf16[128,512]{1,0:T(8,128)(2,1)S(1)}, bf16[128,512]{1,0:T(8,128)(2,1)S(1)}, u32[]{:S(2)}, u32[]{:S(2)}) %collective-permute-start.16) | collective-permute-done | bytes 131104 | tf_op jit(solution)/shard_map/ppermute | solution.py:47
  41.2 2.4 collective-permute-done.8.refs_3_.refs_7_
  44.0 3.2 %collective-permute-done.17.refs_1_.refs_6_ = bf16[128,512]{1,0:T(8,128)(2,1)S(1)} collective-permute-done((bf16[128,512]{1,0:T(8,128)(2,1)S(1)}, bf16[128,512]{1,0:T(8,128)(2,1)S(1)}, u32[]{:S(2)}, u32[]{:S(2)}) %collective-permute-start.17) | collective-permute-done | bytes 131104 | tf_op jit(solution)/shard_map/ppermute | solution.py:47
  47.2 1.4 collective-permute-done.9.refs_3_.refs_1_
  49.4 1.7 collective-permute-start.25
  54.2 1.7 collective-permute-start.27
  59.5 3.1 %collective-permute-start.26 = (f16[128,1024]{1,0:T(8,128)(2,1)}, f16[128,1024]{1,0:T(8,128)(2,1)}, u32[]{:S(2)}, u32[]{:S(2)}) collective-permute-start(f16[128,1024]{1,0:T(8,128)(2,1)} %add_convert_fusion.5), channel_id=1, source_target_pairs={{0,24},{2,26},{4,28},{6,30},{8,0},{10,2},{12,4},{14,6},{16,8},{18,... | collective-permute-start | bytes 786440 | tf_op jit(solution)/shard_map/ppermute | solution.py:43
  62.6 1.6 collective-permute-done.23
  65.3 4.6 %collective-permute-done.21 = f16[128,1024]{1,0:T(8,128)(2,1)S(1)} collective-permute-done((f16[128,1024]{1,0:T(8,128)(2,1)S(1)}, f16[128,1024]{1,0:T(8,128)(2,1)S(1)}, u32[]{:S(2)}, u32[]{:S(2)}) %collective-permute-start.21) | collective-permute-done | bytes 262176 | tf_op jit(solution)/shard_map/ppermute | solution.py:38
  71.5 4.6 %collective-permute-done.24 = f16[128,1024]{1,0:T(8,128)(2,1)} collective-permute-done((f16[128,1024]{1,0:T(8,128)(2,1)}, f16[128,1024]{1,0:T(8,128)(2,1)}, u32[]{:S(2)}, u32[]{:S(2)}) %collective-permute-start.24) | collective-permute-done | bytes 262176 | tf_op jit(solution)/shard_map/ppermute | solution.py:43
  76.1 6.9 %collective-permute-done.22 = f16[128,1024]{1,0:T(8,128)(2,1)} collective-permute-done((f16[128,1024]{1,0:T(8,128)(2,1)}, f16[128,1024]{1,0:T(8,128)(2,1)}, u32[]{:S(2)}, u32[]{:S(2)}) %collective-permute-start.22) | collective-permute-done | bytes 262176 | tf_op jit(solution)/shard_map/ppermute | solution.py:43
  83.0 1.4 convert_add_fusion.refs_0_
  85.4 1.4 pad_maximum_fusion
  88.3 3.5 %collective-permute-start.31 = (bf16[256,512]{1,0:T(8,128)(2,1)S(1)}, bf16[256,512]{1,0:T(8,128)(2,1)S(1)}, u32[]{:S(2)}, u32[]{:S(2)}) collective-permute-start(bf16[256,512]{1,0:T(8,128)(2,1)S(1)} %constant_dynamic-update-slice_fusion.refs_2_), channel_id=1, source_target_pairs={{0,24},{2,26},{4,28},{6,30},{8,0},{10,2},{12,4},{14,6},{16,8},{18,... | collective-permute-start | bytes 786440 | tf_op jit(solution)/shard_map/ppermute | solution.py:43
  91.8 6.9 %collective-permute-done.29.refs_3_ = bf16[256,512]{1,0:T(8,128)(2,1)S(1)} collective-permute-done((bf16[256,512]{1,0:T(8,128)(2,1)S(1)}, bf16[256,512]{1,0:T(8,128)(2,1)S(1)}, u32[]{:S(2)}, u32[]{:S(2)}) %collective-permute-start.29) | collective-permute-done | bytes 262176 | tf_op jit(solution)/shard_map/ppermute | solution.py:43
  98.8 1.5 collective-permute-start.32
  100.9 1.5 collective-permute-done.31.refs_5_
  102.3 1.4 collective-permute-start.35
  103.7 5.3 %collective-permute-done.30.refs_4_ = bf16[256,512]{1,0:T(8,128)(2,1)S(1)} collective-permute-done((bf16[256,512]{1,0:T(8,128)(2,1)S(1)}, bf16[256,512]{1,0:T(8,128)(2,1)S(1)}, u32[]{:S(2)}, u32[]{:S(2)}) %collective-permute-start.30) | collective-permute-done | bytes 262176 | tf_op jit(solution)/shard_map/ppermute | solution.py:43
  109.0 1.4 collective-permute-start.34
  110.4 1.4 pad_maximum_fusion.1.refs_0_.refs_1_
  111.8 7.5 %collective-permute-done.35.refs_9_ = bf16[256,512]{1,0:T(8,128)(2,1)S(1)} collective-permute-done((bf16[256,512]{1,0:T(8,128)(2,1)S(1)}, bf16[256,512]{1,0:T(8,128)(2,1)S(1)}, u32[]{:S(2)}, u32[]{:S(2)}) %collective-permute-start.35) | collective-permute-done | bytes 262176 | tf_op jit(solution)/shard_map/ppermute | solution.py:38
  119.3 2.8 %collective-permute-done.34.refs_8_ = bf16[256,512]{1,0:T(8,128)(2,1)S(1)} collective-permute-done((bf16[256,512]{1,0:T(8,128)(2,1)S(1)}, bf16[256,512]{1,0:T(8,128)(2,1)S(1)}, u32[]{:S(2)}, u32[]{:S(2)}) %collective-permute-start.34) | collective-permute-done | bytes 262176 | tf_op jit(solution)/shard_map/ppermute | solution.py:38
  122.2 24.2 %attention.1 = (bf16[512,1024]{1,0:T(8,128)(2,1)S(1)}, bf16[512,1024]{1,0:T(8,128)(2,1)S(1)}, f32[256,512]{1,0:T(8,128)S(1)}, f32[256,512]{1,0:T(8,128)S(1)}, f3...) custom-call(s32[2,16]{1,0:T(2,128)S(1)} %fusion.7.pos_ref, ...), custom_call_target="tpu_custom_call" | custom-call | flops 12884901888 | bytes 9437184 | tf_op jit(solution)/shard_map/attention/pallas_call | solution.py:279
  147.4 13.4 %collective-permute-start.38 = (bf16[256,512]{1,0:T(8,128)(2,1)S(1)}, bf16[256,512]{1,0:T(8,128)(2,1)S(1)}, u32[]{:S(2)}, u32[]{:S(2)}) collective-permute-start(bf16[256,512]{1,0:T(8,128)(2,1)S(1)} %get-tuple-element.80), channel_id=1, source_target_pairs={{0,4},{2,6},{4,0},{6,2},{8,12},{10,14},{12,8},{14,10},{16,20},{18,... | collective-permute-start | bytes 786440 | tf_op jit(solution)/shard_map/ppermute | solution.py:38
  160.9 1.9 collective-permute-start.42
  163.0 1.4 collective-permute-start.37
  164.4 3.5 %collective-permute-done.38 = bf16[256,512]{1,0:T(8,128)(2,1)S(1)} collective-permute-done((bf16[256,512]{1,0:T(8,128)(2,1)S(1)}, bf16[256,512]{1,0:T(8,128)(2,1)S(1)}, u32[]{:S(2)}, u32[]{:S(2)}) %collective-permute-start.38) | collective-permute-done | bytes 262176 | tf_op jit(solution)/shard_map/ppermute | solution.py:38
  168.1 5.5 %collective-permute-done.40 = bf16[256,512]{1,0:T(8,128)(2,1)S(1)} collective-permute-done((bf16[256,512]{1,0:T(8,128)(2,1)S(1)}, bf16[256,512]{1,0:T(8,128)(2,1)S(1)}, u32[]{:S(2)}, u32[]{:S(2)}) %collective-permute-start.40) | collective-permute-done | bytes 262176 | tf_op jit(solution)/shard_map/ppermute | solution.py:38
  173.9 5.3 %collective-permute-done.42 = bf16[256,512]{1,0:T(8,128)(2,1)S(1)} collective-permute-done((bf16[256,512]{1,0:T(8,128)(2,1)S(1)}, bf16[256,512]{1,0:T(8,128)(2,1)S(1)}, u32[]{:S(2)}, u32[]{:S(2)}) %collective-permute-start.42) | collective-permute-done | bytes 262176 | tf_op jit(solution)/shard_map/ppermute | solution.py:38
  179.3 4.6 %collective-permute-done.44.refs_4_ = bf16[256,512]{1,0:T(8,128)(2,1)S(1)} collective-permute-done((bf16[256,512]{1,0:T(8,128)(2,1)S(1)}, bf16[256,512]{1,0:T(8,128)(2,1)S(1)}, u32[]{:S(2)}, u32[]{:S(2)}) %collective-permute-start.44) | collective-permute-done | bytes 262176 | tf_op jit(solution)/shard_map/ppermute | solution.py:38
  184.9 3.9 %collective-permute-done.43.refs_3_ = bf16[256,512]{1,0:T(8,128)(2,1)S(1)} collective-permute-done((bf16[256,512]{1,0:T(8,128)(2,1)S(1)}, bf16[256,512]{1,0:T(8,128)(2,1)S(1)}, u32[]{:S(2)}, u32[]{:S(2)}) %collective-permute-start.43) | collective-permute-done | bytes 262176 | tf_op jit(solution)/shard_map/ppermute | solution.py:43
  189.1 1.5 collective-permute-done.45.refs_1_
  191.3 3.5 %collective-permute-start.49 = (bf16[128,512]{1,0:T(8,128)(2,1)S(1)}, bf16[128,512]{1,0:T(8,128)(2,1)S(1)}, u32[]{:S(2)}, u32[]{:S(2)}) collective-permute-start(bf16[128,512]{1,0:T(8,128)(2,1)S(1)} %get-tuple-element.95.refs_8_), channel_id=1, source_target_pairs={{0,24},{2,26},{4,28},{6,30},{8,0},{10,2},{12,4},{14,6},{16,8},{18,... | collective-permute-start | bytes 393224 | tf_op jit(solution)/shard_map/ppermute | solution.py:43
  194.8 1.9 collective-permute-start.46
  196.7 3.8 %collective-permute-start.55 = (bf16[128,512]{1,0:T(8,128)(2,1)S(1)}, bf16[128,512]{1,0:T(8,128)(2,1)S(1)}, u32[]{:S(2)}, u32[]{:S(2)}) collective-permute-start(bf16[128,512]{1,0:T(8,128)(2,1)S(1)} %get-tuple-element.90.refs_8_), channel_id=1, source_target_pairs={{0,24},{2,26},{4,28},{6,30},{8,0},{10,2},{12,4},{14,6},{16,8},{18,... | collective-permute-start | bytes 393224 | tf_op jit(solution)/shard_map/ppermute | solution.py:43
  200.5 1.6 collective-permute-start.50
  202.1 2.7 %collective-permute-done.47.refs_10_ = bf16[128,512]{1,0:T(8,128)(2,1)S(1)} collective-permute-done((bf16[128,512]{1,0:T(8,128)(2,1)S(1)}, bf16[128,512]{1,0:T(8,128)(2,1)S(1)}, u32[]{:S(2)}, u32[]{:S(2)}) %collective-permute-start.47) | collective-permute-done | bytes 131104 | tf_op jit(solution)/shard_map/ppermute | solution.py:43
  204.8 1.9 collective-permute-start.52
  206.9 3.5 %collective-permute-done.53.refs_12_ = bf16[128,512]{1,0:T(8,128)(2,1)S(1)} collective-permute-done((bf16[128,512]{1,0:T(8,128)(2,1)S(1)}, bf16[128,512]{1,0:T(8,128)(2,1)S(1)}, u32[]{:S(2)}, u32[]{:S(2)}) %collective-permute-start.53) | collective-permute-done | bytes 131104 | tf_op jit(solution)/shard_map/ppermute | solution.py:43
  210.4 1.9 collective-permute-start.54
  212.4 2.9 %collective-permute-done.54.refs_13_ = bf16[128,512]{1,0:T(8,128)(2,1)S(1)} collective-permute-done((bf16[128,512]{1,0:T(8,128)(2,1)S(1)}, bf16[128,512]{1,0:T(8,128)(2,1)S(1)}, u32[]{:S(2)}, u32[]{:S(2)}) %collective-permute-start.54) | collective-permute-done | bytes 131104 | tf_op jit(solution)/shard_map/ppermute | solution.py:38
  218.8 1.4 collective-permute-start.59
  220.2 1.9 collective-permute-start.62
  222.2 1.9 collective-permute-start.61
  224.9 2.3 collective-permute-done.59.refs_2_
  227.9 1.4 collective-permute-done.60.refs_11_
  229.4 1.9 collective-permute-done.61.refs_13_
  232.6 2.1 weight_gradient.6
  238.0 1.6 place_columns.3
  239.5 1.6 place_columns.2
  241.1 3.3 %collective-permute-done.65.refs_5_ = bf16[256,512]{1,0:T(8,128)(2,1)S(1)} collective-permute-done((bf16[256,512]{1,0:T(8,128)(2,1)}, bf16[256,512]{1,0:T(8,128)(2,1)S(1)}, u32[]{:S(2)}, u32[]{:S(2)}) %collective-permute-start.65) | collective-permute-done | bytes 262176 | tf_op jit(solution)/shard_map/ppermute | solution.py:47
  244.5 2.6 %split_heads.1 = (f32[256,1024]{1,0:T(8,128)}, f32[256,1024]{1,0:T(8,128)}) custom-call(s32[1]{0:T(128)} %bitcast.26.index_ref, f32[256,512]{1,0:T(8,128)S(1)} %copy-done.31, f32[256,512]{1,0:T(8,128)S(1)} %copy-done.33, bf16[256,512]{1,0:T(8,128)(2,1)S(1)} %copy-done.37, f32[256,512]{1,0:T(8,128)S(1)} %copy-done.35, ...), custom_call_target="tpu_custom_call" | custom-call | bytes 4718592 | tf_op jit(solution)/shard_map/split_heads/pallas_call | solution.py:302
  (216 shorter events, 35.3 us)
Async XLA Ops:
  2.1 17.0 %collective-permute-start.5 = (bf16[256,1024]{1,0:T(8,128)(2,1)S(1)}, bf16[256,1024]{1,0:T(8,128)(2,1)S(1)}, u32[]{:S(2)}, u32[]{:S(2)}) collective-permute-start(bf16[256,1024]{1,0:T(8,128)(2,1)S(1)} %pad_maximum_fusion.6), channel_id=1, source_target_pairs={{0,1},{1,0},{2,3},{3,2},{4,5},{5,4},{6,7},{7,6},{8,9},{9,8},{10,11... | collective-permute-start | bytes 1572872 | tf_op jit(solution)/shard_map/ppermute | solution.py:47
  5.9 7.5 %collective-permute-start.12 = (bf16[128,512]{1,0:T(8,128)(2,1)S(1)}, bf16[128,512]{1,0:T(8,128)(2,1)S(1)}, u32[]{:S(2)}, u32[]{:S(2)}) collective-permute-start(bf16[128,512]{1,0:T(8,128)(2,1)S(1)} %get-tuple-element.106), channel_id=1, source_target_pairs={{0,8},{2,10},{4,12},{6,14},{8,16},{10,18},{12,20},{14,22},{16,24},... | collective-permute-start | bytes 393224 | tf_op jit(solution)/shard_map/ppermute | solution.py:43
  7.5 10.5 %collective-permute-start.2 = (bf16[128,512]{1,0:T(8,128)(2,1)S(1)}, bf16[128,512]{1,0:T(8,128)(2,1)S(1)}, u32[]{:S(2)}, u32[]{:S(2)}) collective-permute-start(bf16[128,512]{1,0:T(8,128)(2,1)S(1)} %get-tuple-element.109), channel_id=1, source_target_pairs={{0,12},{2,14},{4,8},{6,10},{8,20},{10,22},{12,16},{14,18},{16,28},... | collective-permute-start | bytes 393224 | tf_op jit(solution)/shard_map/ppermute | solution.py:43
  13.4 11.1 %collective-permute-start.13 = (bf16[128,512]{1,0:T(8,128)(2,1)S(1)}, bf16[128,512]{1,0:T(8,128)(2,1)S(1)}, u32[]{:S(2)}, u32[]{:S(2)}) collective-permute-start(bf16[128,512]{1,0:T(8,128)(2,1)S(1)} %get-tuple-element.61), channel_id=1, source_target_pairs={{0,16},{2,18},{4,20},{6,22},{8,24},{10,26},{12,28},{14,30},{16,0},... | collective-permute-start | bytes 393224 | tf_op jit(solution)/shard_map/ppermute | solution.py:43
  18.0 10.3 %collective-permute-start.3 = (bf16[128,512]{1,0:T(8,128)(2,1)S(1)}, bf16[128,512]{1,0:T(8,128)(2,1)S(1)}, u32[]{:S(2)}, u32[]{:S(2)}) collective-permute-start(bf16[128,512]{1,0:T(8,128)(2,1)S(1)} %get-tuple-element.53), channel_id=1, source_target_pairs={{0,20},{2,22},{4,16},{6,18},{8,28},{10,30},{12,24},{14,26},{16,4},... | collective-permute-start | bytes 393224 | tf_op jit(solution)/shard_map/ppermute | solution.py:43
  19.1 10.2 %collective-permute-start.6 = (bf16[128,512]{1,0:T(8,128)(2,1)S(1)}, bf16[128,512]{1,0:T(8,128)(2,1)S(1)}, u32[]{:S(2)}, u32[]{:S(2)}) collective-permute-start(bf16[128,512]{1,0:T(8,128)(2,1)S(1)} %collective-permute-done.2.refs_2_.refs_3_), channel_id=1, source_target_pairs={{0,1},{1,0},{2,3},{3,2},{4,5},{5,4},{6,7},{7,6},{8,9},{9,8},{10,11... | collective-permute-start | bytes 393224 | tf_op jit(solution)/shard_map/ppermute | solution.py:47
  19.6 10.4 %collective-permute-start.15 = (bf16[128,512]{1,0:T(8,128)(2,1)S(1)}, bf16[128,512]{1,0:T(8,128)(2,1)S(1)}, u32[]{:S(2)}, u32[]{:S(2)}) collective-permute-start(bf16[128,512]{1,0:T(8,128)(2,1)S(1)} %collective-permute-done.12.refs_0_.refs_2_), channel_id=1, source_target_pairs={{0,1},{1,0},{2,3},{3,2},{4,5},{5,4},{6,7},{7,6},{8,9},{9,8},{10,11... | collective-permute-start | bytes 393224 | tf_op jit(solution)/shard_map/ppermute | solution.py:47
  24.5 10.9 %collective-permute-start.14 = (bf16[128,512]{1,0:T(8,128)(2,1)}, bf16[128,512]{1,0:T(8,128)(2,1)S(1)}, u32[]{:S(2)}, u32[]{:S(2)}) collective-permute-start(bf16[128,512]{1,0:T(8,128)(2,1)} %get-tuple-element.62), channel_id=1, source_target_pairs={{0,24},{2,26},{4,28},{6,30},{8,0},{10,2},{12,4},{14,6},{16,8},{18,... | collective-permute-start | bytes 393224 | tf_op jit(solution)/shard_map/ppermute | solution.py:43
  28.3 6.1 %collective-permute-start.4 = (bf16[128,512]{1,0:T(8,128)(2,1)}, bf16[128,512]{1,0:T(8,128)(2,1)S(1)}, u32[]{:S(2)}, u32[]{:S(2)}) collective-permute-start(bf16[128,512]{1,0:T(8,128)(2,1)} %get-tuple-element.54), channel_id=1, source_target_pairs={{0,28},{2,30},{4,24},{6,26},{8,4},{10,6},{12,0},{14,2},{16,12},{18... | collective-permute-start | bytes 393224 | tf_op jit(solution)/shard_map/ppermute | solution.py:43
  29.3 5.5 %collective-permute-start.7 = (bf16[128,512]{1,0:T(8,128)(2,1)S(1)}, bf16[128,512]{1,0:T(8,128)(2,1)S(1)}, u32[]{:S(2)}, u32[]{:S(2)}) collective-permute-start(bf16[128,512]{1,0:T(8,128)(2,1)S(1)} %collective-permute-done.3.refs_2_.refs_5_), channel_id=1, source_target_pairs={{0,1},{1,0},{2,3},{3,2},{4,5},{5,4},{6,7},{7,6},{8,9},{9,8},{10,11... | collective-permute-start | bytes 393224 | tf_op jit(solution)/shard_map/ppermute | solution.py:47
  29.9 18.7 %collective-permute-start.19 = (bf16[256,1024]{1,0:T(8,128)(2,1)S(1)}, bf16[256,1024]{1,0:T(8,128)(2,1)S(1)}, u32[]{:S(2)}, u32[]{:S(2)}) collective-permute-start(bf16[256,1024]{1,0:T(8,128)(2,1)S(1)} %pad_maximum_fusion.7.refs_4_), channel_id=1, source_target_pairs={{0,2},{2,0},{4,6},{6,4},{8,10},{10,8},{12,14},{14,12},{16,18},{18,... | collective-permute-start | bytes 1572872 | tf_op jit(solution)/shard_map/ppermute | solution.py:33
  30.0 18.6 %collective-permute-start.20 = (bf16[256,1024]{1,0:T(8,128)(2,1)S(1)}, bf16[256,1024]{1,0:T(8,128)(2,1)S(1)}, u32[]{:S(2)}, u32[]{:S(2)}) collective-permute-start(bf16[256,1024]{1,0:T(8,128)(2,1)S(1)} %collective-permute-done.5.refs_6_), channel_id=1, source_target_pairs={{0,2},{2,0},{4,6},{6,4},{8,10},{10,8},{12,14},{14,12},{16,18},{18,... | collective-permute-start | bytes 1572872 | tf_op jit(solution)/shard_map/ppermute | solution.py:33
  34.4 6.8 %collective-permute-start.1 = (bf16[128,512]{1,0:T(8,128)(2,1)S(1)}, bf16[128,512]{1,0:T(8,128)(2,1)S(1)}, u32[]{:S(2)}, u32[]{:S(2)}) collective-permute-start(bf16[128,512]{1,0:T(8,128)(2,1)S(1)} %get-tuple-element.112), channel_id=1, source_target_pairs={{0,4},{2,6},{4,0},{6,2},{8,12},{10,14},{12,8},{14,10},{16,20},{18,... | collective-permute-start | bytes 393224 | tf_op jit(solution)/shard_map/ppermute | solution.py:43
  34.9 5.9 %collective-permute-start.16 = (bf16[128,512]{1,0:T(8,128)(2,1)S(1)}, bf16[128,512]{1,0:T(8,128)(2,1)S(1)}, u32[]{:S(2)}, u32[]{:S(2)}) collective-permute-start(bf16[128,512]{1,0:T(8,128)(2,1)S(1)} %collective-permute-done.13.refs_0_.refs_4_), channel_id=1, source_target_pairs={{0,1},{1,0},{2,3},{3,2},{4,5},{5,4},{6,7},{7,6},{8,9},{9,8},{10,11... | collective-permute-start | bytes 393224 | tf_op jit(solution)/shard_map/ppermute | solution.py:47
  35.4 8.2 %collective-permute-start.8 = (bf16[128,512]{1,0:T(8,128)(2,1)S(1)}, bf16[128,512]{1,0:T(8,128)(2,1)S(1)}, u32[]{:S(2)}, u32[]{:S(2)}) collective-permute-start(bf16[128,512]{1,0:T(8,128)(2,1)S(1)} %collective-permute-done.4.refs_2_.refs_7_), channel_id=1, source_target_pairs={{0,1},{1,0},{2,3},{3,2},{4,5},{5,4},{6,7},{7,6},{8,9},{9,8},{10,11... | collective-permute-start | bytes 393224 | tf_op jit(solution)/shard_map/ppermute | solution.py:47
  40.8 6.4 %collective-permute-start.17 = (bf16[128,512]{1,0:T(8,128)(2,1)S(1)}, bf16[128,512]{1,0:T(8,128)(2,1)S(1)}, u32[]{:S(2)}, u32[]{:S(2)}) collective-permute-start(bf16[128,512]{1,0:T(8,128)(2,1)S(1)} %collective-permute-done.14.refs_0_.refs_6_), channel_id=1, source_target_pairs={{0,1},{1,0},{2,3},{3,2},{4,5},{5,4},{6,7},{7,6},{8,9},{9,8},{10,11... | collective-permute-start | bytes 393224 | tf_op jit(solution)/shard_map/ppermute | solution.py:47
  43.6 5.0 %collective-permute-start.9 = (bf16[128,512]{1,0:T(8,128)(2,1)S(1)}, bf16[128,512]{1,0:T(8,128)(2,1)S(1)}, u32[]{:S(2)}, u32[]{:S(2)}) collective-permute-start(bf16[128,512]{1,0:T(8,128)(2,1)S(1)} %collective-permute-done.1.refs_2_.refs_1_), channel_id=1, source_target_pairs={{0,1},{1,0},{2,3},{3,2},{4,5},{5,4},{6,7},{7,6},{8,9},{9,8},{10,11... | collective-permute-start | bytes 393224 | tf_op jit(solution)/shard_map/ppermute | solution.py:47
  47.2 6.2 %collective-permute-start.18 = (bf16[128,512]{1,0:T(8,128)(2,1)S(1)}, bf16[128,512]{1,0:T(8,128)(2,1)S(1)}, u32[]{:S(2)}, u32[]{:S(2)}) collective-permute-start(bf16[128,512]{1,0:T(8,128)(2,1)S(1)} %get-tuple-element.65.refs_0_), channel_id=1, source_target_pairs={{0,1},{1,0},{2,3},{3,2},{4,5},{5,4},{6,7},{7,6},{8,9},{9,8},{10,11... | collective-permute-start | bytes 393224 | tf_op jit(solution)/shard_map/ppermute | solution.py:47
  49.4 9.3 %collective-permute-start.25 = (f16[128,1024]{1,0:T(8,128)(2,1)S(1)}, f16[128,1024]{1,0:T(8,128)(2,1)S(1)}, u32[]{:S(2)}, u32[]{:S(2)}) collective-permute-start(f16[128,1024]{1,0:T(8,128)(2,1)S(1)} %convert_element_type.86), channel_id=1, source_target_pairs={{0,4},{2,6},{4,0},{6,2},{8,12},{10,14},{12,8},{14,10},{16,20},{18,... | collective-permute-start | bytes 786440 | tf_op jit(solution)/shard_map/ppermute | solution.py:38
  52.0 12.3 %collective-permute-start.23 = (f16[128,1024]{1,0:T(8,128)(2,1)S(1)}, f16[128,1024]{1,0:T(8,128)(2,1)S(1)}, u32[]{:S(2)}, u32[]{:S(2)}) collective-permute-start(f16[128,1024]{1,0:T(8,128)(2,1)S(1)} %convert_element_type.82), channel_id=1, source_target_pairs={{0,4},{2,6},{4,0},{6,2},{8,12},{10,14},{12,8},{14,10},{16,20},{18,... | collective-permute-start | bytes 786440 | tf_op jit(solution)/shard_map/ppermute | solution.py:38
  54.2 17.2 %collective-permute-start.27 = (f16[128,1024]{1,0:T(8,128)(2,1)S(1)}, f16[128,1024]{1,0:T(8,128)(2,1)}, u32[]{:S(2)}, u32[]{:S(2)}) collective-permute-start(f16[128,1024]{1,0:T(8,128)(2,1)S(1)} %convert_element_type.90), channel_id=1, source_target_pairs={{0,4},{2,6},{4,0},{6,2},{8,12},{10,14},{12,8},{14,10},{16,20},{18,... | collective-permute-start | bytes 786440 | tf_op jit(solution)/shard_map/ppermute | solution.py:38
  55.9 14.0 %collective-permute-start.21 = (f16[128,1024]{1,0:T(8,128)(2,1)S(1)}, f16[128,1024]{1,0:T(8,128)(2,1)S(1)}, u32[]{:S(2)}, u32[]{:S(2)}) collective-permute-start(f16[128,1024]{1,0:T(8,128)(2,1)S(1)} %convert_element_type.78), channel_id=1, source_target_pairs={{0,4},{2,6},{4,0},{6,2},{8,12},{10,14},{12,8},{14,10},{16,20},{18,... | collective-permute-start | bytes 786440 | tf_op jit(solution)/shard_map/ppermute | solution.py:38
  56.6 28.7 %collective-permute-start.10 = (bf16[128,4096]{1,0:T(8,128)(2,1)S(1)}, bf16[128,4096]{1,0:T(8,128)(2,1)}, u32[]{:S(2)}, u32[]{:S(2)}) collective-permute-start(bf16[128,4096]{1,0:T(8,128)(2,1)S(1)} %pad_maximum_fusion.2), channel_id=1, source_target_pairs={{0,1},{1,0},{2,3},{3,2},{4,5},{5,4},{6,7},{7,6},{8,9},{9,8},{10,11... | collective-permute-start | bytes 3145736 | tf_op jit(solution)/shard_map/ppermute | solution.py:47
  59.5 12.0 %collective-permute-start.26 = (f16[128,1024]{1,0:T(8,128)(2,1)}, f16[128,1024]{1,0:T(8,128)(2,1)}, u32[]{:S(2)}, u32[]{:S(2)}) collective-permute-start(f16[128,1024]{1,0:T(8,128)(2,1)} %add_convert_fusion.5), channel_id=1, source_target_pairs={{0,24},{2,26},{4,28},{6,30},{8,0},{10,2},{12,4},{14,6},{16,8},{18,... | collective-permute-start | bytes 786440 | tf_op jit(solution)/shard_map/ppermute | solution.py:43
  65.0 11.1 %collective-permute-start.24 = (f16[128,1024]{1,0:T(8,128)(2,1)}, f16[128,1024]{1,0:T(8,128)(2,1)}, u32[]{:S(2)}, u32[]{:S(2)}) collective-permute-start(f16[128,1024]{1,0:T(8,128)(2,1)} %add_convert_fusion.6), channel_id=1, source_target_pairs={{0,8},{2,10},{4,12},{6,14},{8,16},{10,18},{12,20},{14,22},{16,24},... | collective-permute-start | bytes 786440 | tf_op jit(solution)/shard_map/ppermute | solution.py:43
  70.6 12.3 %collective-permute-start.22 = (f16[128,1024]{1,0:T(8,128)(2,1)}, f16[128,1024]{1,0:T(8,128)(2,1)}, u32[]{:S(2)}, u32[]{:S(2)}) collective-permute-start(f16[128,1024]{1,0:T(8,128)(2,1)} %add_convert_fusion.7), channel_id=1, source_target_pairs={{0,16},{2,18},{4,20},{6,22},{8,24},{10,26},{12,28},{14,30},{16,0},... | collective-permute-start | bytes 786440 | tf_op jit(solution)/shard_map/ppermute | solution.py:43
  85.3 2.3 collective-permute-start.28
  87.0 23.4 %collective-permute-start.11 = (bf16[256,2048]{1,0:T(8,128)(2,1)S(1)}, bf16[256,2048]{1,0:T(8,128)(2,1)}, u32[]{:S(2)}, u32[]{:S(2)}) collective-permute-start(bf16[256,2048]{1,0:T(8,128)(2,1)S(1)} %pad_maximum_fusion.3), channel_id=1, source_target_pairs={{0,2},{2,0},{4,6},{6,4},{8,10},{10,8},{12,14},{14,12},{16,18},{18,... | collective-permute-start | bytes 3145736 | tf_op jit(solution)/shard_map/ppermute | solution.py:33
  87.7 11.1 %collective-permute-start.29 = (bf16[256,512]{1,0:T(8,128)(2,1)S(1)}, bf16[256,512]{1,0:T(8,128)(2,1)S(1)}, u32[]{:S(2)}, u32[]{:S(2)}) collective-permute-start(bf16[256,512]{1,0:T(8,128)(2,1)S(1)} %constant_dynamic-update-slice_fusion.refs_2_), channel_id=1, source_target_pairs={{0,8},{2,10},{4,12},{6,14},{8,16},{10,18},{12,20},{14,22},{16,24},... | collective-permute-start | bytes 786440 | tf_op jit(solution)/shard_map/ppermute | solution.py:43
  87.9 10.9 %collective-permute-start = (s32[1,2,16]{2,1,0:T(2,128)S(1)}, s32[1,2,16]{2,1,0:T(2,128)S(1)}, u32[]{:S(2)}, u32[]{:S(2)}) collective-permute-start(s32[1,2,16]{2,1,0:T(2,128)S(1)} %bitcast.49), channel_id=1, source_target_pairs={{0,2},{2,0},{4,6},{6,4},{8,10},{10,8},{12,14},{14,12},{16,18},{18,... | collective-permute-start | bytes 392 | tf_op jit(solution)/shard_map/ppermute | solution.py:33
  88.3 14.0 %collective-permute-start.31 = (bf16[256,512]{1,0:T(8,128)(2,1)S(1)}, bf16[256,512]{1,0:T(8,128)(2,1)S(1)}, u32[]{:S(2)}, u32[]{:S(2)}) collective-permute-start(bf16[256,512]{1,0:T(8,128)(2,1)S(1)} %constant_dynamic-update-slice_fusion.refs_2_), channel_id=1, source_target_pairs={{0,24},{2,26},{4,28},{6,30},{8,0},{10,2},{12,4},{14,6},{16,8},{18,... | collective-permute-start | bytes 786440 | tf_op jit(solution)/shard_map/ppermute | solution.py:43
  98.7 10.3 %collective-permute-start.30 = (bf16[256,512]{1,0:T(8,128)(2,1)S(1)}, bf16[256,512]{1,0:T(8,128)(2,1)S(1)}, u32[]{:S(2)}, u32[]{:S(2)}) collective-permute-start(bf16[256,512]{1,0:T(8,128)(2,1)S(1)} %collective-permute-done.29.refs_3_), channel_id=1, source_target_pairs={{0,8},{2,10},{4,12},{6,14},{8,16},{10,18},{12,20},{14,22},{16,24},... | collective-permute-start | bytes 786440 | tf_op jit(solution)/shard_map/ppermute | solution.py:43
  98.8 13.0 %collective-permute-start.32 = (bf16[256,512]{1,0:T(8,128)(2,1)S(1)}, bf16[256,512]{1,0:T(8,128)(2,1)S(1)}, u32[]{:S(2)}, u32[]{:S(2)}) collective-permute-start(bf16[256,512]{1,0:T(8,128)(2,1)S(1)} %constant_dynamic-update-slice_fusion.refs_2_), channel_id=1, source_target_pairs={{0,4},{2,6},{4,0},{6,2},{8,12},{10,14},{12,8},{14,10},{16,20},{18,... | collective-permute-start | bytes 786440 | tf_op jit(solution)/shard_map/ppermute | solution.py:38
  100.2 19.1 %collective-permute-start.33 = (bf16[256,512]{1,0:T(8,128)(2,1)S(1)}, bf16[256,512]{1,0:T(8,128)(2,1)S(1)}, u32[]{:S(2)}, u32[]{:S(2)}) collective-permute-start(bf16[256,512]{1,0:T(8,128)(2,1)S(1)} %collective-permute-done.29.refs_3_), channel_id=1, source_target_pairs={{0,4},{2,6},{4,0},{6,2},{8,12},{10,14},{12,8},{14,10},{16,20},{18,... | collective-permute-start | bytes 786440 | tf_op jit(solution)/shard_map/ppermute | solution.py:38
  102.3 17.0 %collective-permute-start.35 = (bf16[256,512]{1,0:T(8,128)(2,1)S(1)}, bf16[256,512]{1,0:T(8,128)(2,1)S(1)}, u32[]{:S(2)}, u32[]{:S(2)}) collective-permute-start(bf16[256,512]{1,0:T(8,128)(2,1)S(1)} %collective-permute-done.31.refs_5_), channel_id=1, source_target_pairs={{0,4},{2,6},{4,0},{6,2},{8,12},{10,14},{12,8},{14,10},{16,20},{18,... | collective-permute-start | bytes 786440 | tf_op jit(solution)/shard_map/ppermute | solution.py:38
  109.0 13.1 %collective-permute-start.34 = (bf16[256,512]{1,0:T(8,128)(2,1)S(1)}, bf16[256,512]{1,0:T(8,128)(2,1)S(1)}, u32[]{:S(2)}, u32[]{:S(2)}) collective-permute-start(bf16[256,512]{1,0:T(8,128)(2,1)S(1)} %collective-permute-done.30.refs_4_), channel_id=1, source_target_pairs={{0,4},{2,6},{4,0},{6,2},{8,12},{10,14},{12,8},{14,10},{16,20},{18,... | collective-permute-start | bytes 786440 | tf_op jit(solution)/shard_map/ppermute | solution.py:38
  146.5 16.3 %collective-permute-start.36 = (bf16[256,2048]{1,0:T(8,128)(2,1)S(1)}, bf16[256,2048]{1,0:T(8,128)(2,1)S(1)}, u32[]{:S(2)}, u32[]{:S(2)}) collective-permute-start(bf16[256,2048]{1,0:T(8,128)(2,1)S(1)} %pad_maximum_fusion.4), channel_id=1, source_target_pairs={{0,2},{2,0},{4,6},{6,4},{8,10},{10,8},{12,14},{14,12},{16,18},{18,... | collective-permute-start | bytes 3145736 | tf_op jit(solution)/shard_map/ppermute | solution.py:33
  147.4 20.6 %collective-permute-start.38 = (bf16[256,512]{1,0:T(8,128)(2,1)S(1)}, bf16[256,512]{1,0:T(8,128)(2,1)S(1)}, u32[]{:S(2)}, u32[]{:S(2)}) collective-permute-start(bf16[256,512]{1,0:T(8,128)(2,1)S(1)} %get-tuple-element.80), channel_id=1, source_target_pairs={{0,4},{2,6},{4,0},{6,2},{8,12},{10,14},{12,8},{14,10},{16,20},{18,... | collective-permute-start | bytes 786440 | tf_op jit(solution)/shard_map/ppermute | solution.py:38
  160.8 12.8 %collective-permute-start.40 = (bf16[256,512]{1,0:T(8,128)(2,1)S(1)}, bf16[256,512]{1,0:T(8,128)(2,1)S(1)}, u32[]{:S(2)}, u32[]{:S(2)}) collective-permute-start(bf16[256,512]{1,0:T(8,128)(2,1)S(1)} %get-tuple-element.82), channel_id=1, source_target_pairs={{0,4},{2,6},{4,0},{6,2},{8,12},{10,14},{12,8},{14,10},{16,20},{18,... | collective-permute-start | bytes 786440 | tf_op jit(solution)/shard_map/ppermute | solution.py:38
  160.9 18.3 %collective-permute-start.42 = (bf16[256,512]{1,0:T(8,128)(2,1)S(1)}, bf16[256,512]{1,0:T(8,128)(2,1)S(1)}, u32[]{:S(2)}, u32[]{:S(2)}) collective-permute-start(bf16[256,512]{1,0:T(8,128)(2,1)S(1)} %get-tuple-element.84), channel_id=1, source_target_pairs={{0,4},{2,6},{4,0},{6,2},{8,12},{10,14},{12,8},{14,10},{16,20},{18,... | collective-permute-start | bytes 786440 | tf_op jit(solution)/shard_map/ppermute | solution.py:38
  162.8 21.1 %collective-permute-start.44 = (bf16[256,512]{1,0:T(8,128)(2,1)S(1)}, bf16[256,512]{1,0:T(8,128)(2,1)S(1)}, u32[]{:S(2)}, u32[]{:S(2)}) collective-permute-start(bf16[256,512]{1,0:T(8,128)(2,1)S(1)} %get-tuple-element.85), channel_id=1, source_target_pairs={{0,4},{2,6},{4,0},{6,2},{8,12},{10,14},{12,8},{14,10},{16,20},{18,... | collective-permute-start | bytes 786440 | tf_op jit(solution)/shard_map/ppermute | solution.py:38
  163.0 27.9 %collective-permute-start.37 = (bf16[128,4096]{1,0:T(8,128)(2,1)S(1)}, bf16[128,4096]{1,0:T(8,128)(2,1)S(1)}, u32[]{:S(2)}, u32[]{:S(2)}) collective-permute-start(bf16[128,4096]{1,0:T(8,128)(2,1)S(1)} %pad_maximum_fusion.5), channel_id=1, source_target_pairs={{0,1},{1,0},{2,3},{3,2},{4,5},{5,4},{6,7},{7,6},{8,9},{9,8},{10,11... | collective-permute-start | bytes 3145736 | tf_op jit(solution)/shard_map/ppermute | solution.py:47
  168.0 15.9 %collective-permute-start.39 = (bf16[256,512]{1,0:T(8,128)(2,1)S(1)}, bf16[256,512]{1,0:T(8,128)(2,1)S(1)}, u32[]{:S(2)}, u32[]{:S(2)}) collective-permute-start(bf16[256,512]{1,0:T(8,128)(2,1)S(1)} %add_convert_fusion.4), channel_id=1, source_target_pairs={{0,16},{2,18},{4,20},{6,22},{8,24},{10,26},{12,28},{14,30},{16,0},... | collective-permute-start | bytes 786440 | tf_op jit(solution)/shard_map/ppermute | solution.py:43
  173.6 11.3 %collective-permute-start.41 = (bf16[256,512]{1,0:T(8,128)(2,1)S(1)}, bf16[256,512]{1,0:T(8,128)(2,1)S(1)}, u32[]{:S(2)}, u32[]{:S(2)}) collective-permute-start(bf16[256,512]{1,0:T(8,128)(2,1)S(1)} %add_convert_fusion.3), channel_id=1, source_target_pairs={{0,8},{2,10},{4,12},{6,14},{8,16},{10,18},{12,20},{14,22},{16,24},... | collective-permute-start | bytes 786440 | tf_op jit(solution)/shard_map/ppermute | solution.py:43
  179.3 9.6 %collective-permute-start.43 = (bf16[256,512]{1,0:T(8,128)(2,1)S(1)}, bf16[256,512]{1,0:T(8,128)(2,1)S(1)}, u32[]{:S(2)}, u32[]{:S(2)}) collective-permute-start(bf16[256,512]{1,0:T(8,128)(2,1)S(1)} %add_convert_fusion.2), channel_id=1, source_target_pairs={{0,24},{2,26},{4,28},{6,30},{8,0},{10,2},{12,4},{14,6},{16,8},{18,... | collective-permute-start | bytes 786440 | tf_op jit(solution)/shard_map/ppermute | solution.py:43
  190.9 9.6 %collective-permute-start.51 = (bf16[128,512]{1,0:T(8,128)(2,1)S(1)}, bf16[128,512]{1,0:T(8,128)(2,1)S(1)}, u32[]{:S(2)}, u32[]{:S(2)}) collective-permute-start(bf16[128,512]{1,0:T(8,128)(2,1)S(1)} %get-tuple-element.90.refs_8_), channel_id=1, source_target_pairs={{0,8},{2,10},{4,12},{6,14},{8,16},{10,18},{12,20},{14,22},{16,24},... | collective-permute-start | bytes 393224 | tf_op jit(solution)/shard_map/ppermute | solution.py:43
  191.3 9.2 %collective-permute-start.49 = (bf16[128,512]{1,0:T(8,128)(2,1)S(1)}, bf16[128,512]{1,0:T(8,128)(2,1)S(1)}, u32[]{:S(2)}, u32[]{:S(2)}) collective-permute-start(bf16[128,512]{1,0:T(8,128)(2,1)S(1)} %get-tuple-element.95.refs_8_), channel_id=1, source_target_pairs={{0,24},{2,26},{4,28},{6,30},{8,0},{10,2},{12,4},{14,6},{16,8},{18,... | collective-permute-start | bytes 393224 | tf_op jit(solution)/shard_map/ppermute | solution.py:43
  194.8 10.0 %collective-permute-start.47 = (bf16[128,512]{1,0:T(8,128)(2,1)S(1)}, bf16[128,512]{1,0:T(8,128)(2,1)S(1)}, u32[]{:S(2)}, u32[]{:S(2)}) collective-permute-start(bf16[128,512]{1,0:T(8,128)(2,1)S(1)} %get-tuple-element.95.refs_8_), channel_id=1, source_target_pairs={{0,8},{2,10},{4,12},{6,14},{8,16},{10,18},{12,20},{14,22},{16,24},... | collective-permute-start | bytes 393224 | tf_op jit(solution)/shard_map/ppermute | solution.py:43
  194.8 10.0 %collective-permute-start.46 = (bf16[128,512]{1,0:T(8,128)(2,1)S(1)}, bf16[128,512]{1,0:T(8,128)(2,1)S(1)}, u32[]{:S(2)}, u32[]{:S(2)}) collective-permute-start(bf16[128,512]{1,0:T(8,128)(2,1)S(1)} %get-tuple-element.95.refs_8_), channel_id=1, source_target_pairs={{0,4},{2,6},{4,0},{6,2},{8,12},{10,14},{12,8},{14,10},{16,20},{18,... | collective-permute-start | bytes 393224 | tf_op jit(solution)/shard_map/ppermute | solution.py:38
  196.7 10.0 %collective-permute-start.55 = (bf16[128,512]{1,0:T(8,128)(2,1)S(1)}, bf16[128,512]{1,0:T(8,128)(2,1)S(1)}, u32[]{:S(2)}, u32[]{:S(2)}) collective-permute-start(bf16[128,512]{1,0:T(8,128)(2,1)S(1)} %get-tuple-element.90.refs_8_), channel_id=1, source_target_pairs={{0,24},{2,26},{4,28},{6,30},{8,0},{10,2},{12,4},{14,6},{16,8},{18,... | collective-permute-start | bytes 393224 | tf_op jit(solution)/shard_map/ppermute | solution.py:43
  200.5 9.9 %collective-permute-start.53 = (bf16[128,512]{1,0:T(8,128)(2,1)S(1)}, bf16[128,512]{1,0:T(8,128)(2,1)S(1)}, u32[]{:S(2)}, u32[]{:S(2)}) collective-permute-start(bf16[128,512]{1,0:T(8,128)(2,1)S(1)} %collective-permute-done.51.refs_10_), channel_id=1, source_target_pairs={{0,8},{2,10},{4,12},{6,14},{8,16},{10,18},{12,20},{14,22},{16,24},... | collective-permute-start | bytes 393224 | tf_op jit(solution)/shard_map/ppermute | solution.py:43
  200.5 11.9 %collective-permute-start.50 = (bf16[128,512]{1,0:T(8,128)(2,1)S(1)}, bf16[128,512]{1,0:T(8,128)(2,1)S(1)}, u32[]{:S(2)}, u32[]{:S(2)}) collective-permute-start(bf16[128,512]{1,0:T(8,128)(2,1)S(1)} %get-tuple-element.90.refs_8_), channel_id=1, source_target_pairs={{0,4},{2,6},{4,0},{6,2},{8,12},{10,14},{12,8},{14,10},{16,20},{18,... | collective-permute-start | bytes 393224 | tf_op jit(solution)/shard_map/ppermute | solution.py:38
  204.8 7.6 %collective-permute-start.48 = (bf16[128,512]{1,0:T(8,128)(2,1)S(1)}, bf16[128,512]{1,0:T(8,128)(2,1)S(1)}, u32[]{:S(2)}, u32[]{:S(2)}) collective-permute-start(bf16[128,512]{1,0:T(8,128)(2,1)S(1)} %collective-permute-done.47.refs_10_), channel_id=1, source_target_pairs={{0,8},{2,10},{4,12},{6,14},{8,16},{10,18},{12,20},{14,22},{16,24},... | collective-permute-start | bytes 393224 | tf_op jit(solution)/shard_map/ppermute | solution.py:43
  204.8 7.6 %collective-permute-start.52 = (bf16[128,512]{1,0:T(8,128)(2,1)S(1)}, bf16[128,512]{1,0:T(8,128)(2,1)S(1)}, u32[]{:S(2)}, u32[]{:S(2)}) collective-permute-start(bf16[128,512]{1,0:T(8,128)(2,1)S(1)} %collective-permute-done.51.refs_10_), channel_id=1, source_target_pairs={{0,4},{2,6},{4,0},{6,2},{8,12},{10,14},{12,8},{14,10},{16,20},{18,... | collective-permute-start | bytes 393224 | tf_op jit(solution)/shard_map/ppermute | solution.py:38
  206.7 5.7 %collective-permute-start.56 = (bf16[128,512]{1,0:T(8,128)(2,1)S(1)}, bf16[128,512]{1,0:T(8,128)(2,1)S(1)}, u32[]{:S(2)}, u32[]{:S(2)}) collective-permute-start(bf16[128,512]{1,0:T(8,128)(2,1)S(1)} %collective-permute-done.55.refs_14_), channel_id=1, source_target_pairs={{0,4},{2,6},{4,0},{6,2},{8,12},{10,14},{12,8},{14,10},{16,20},{18,... | collective-permute-start | bytes 393224 | tf_op jit(solution)/shard_map/ppermute | solution.py:38
  210.4 5.0 %collective-permute-start.54 = (bf16[128,512]{1,0:T(8,128)(2,1)S(1)}, bf16[128,512]{1,0:T(8,128)(2,1)S(1)}, u32[]{:S(2)}, u32[]{:S(2)}) collective-permute-start(bf16[128,512]{1,0:T(8,128)(2,1)S(1)} %collective-permute-done.53.refs_12_), channel_id=1, source_target_pairs={{0,4},{2,6},{4,0},{6,2},{8,12},{10,14},{12,8},{14,10},{16,20},{18,... | collective-permute-start | bytes 393224 | tf_op jit(solution)/shard_map/ppermute | solution.py:38
  218.2 5.9 %collective-permute-start.57 = (f32[256,512]{1,0:T(8,128)S(1)}, f32[256,512]{1,0:T(8,128)S(1)}, u32[]{:S(2)}, u32[]{:S(2)}) collective-permute-start(f32[256,512]{1,0:T(8,128)S(1)} %get-tuple-element.92), channel_id=1, source_target_pairs={{0,2},{2,0},{4,6},{6,4},{8,10},{10,8},{12,14},{14,12},{16,18},{18,... | collective-permute-start | bytes 1572872 | tf_op jit(solution)/shard_map/ppermute | solution.py:33
  218.8 8.4 %collective-permute-start.59 = (bf16[256,512]{1,0:T(8,128)(2,1)S(1)}, bf16[256,512]{1,0:T(8,128)(2,1)S(1)}, u32[]{:S(2)}, u32[]{:S(2)}) collective-permute-start(bf16[256,512]{1,0:T(8,128)(2,1)S(1)} %add_convert_fusion.1), channel_id=1, source_target_pairs={{0,1},{1,0},{2,3},{3,2},{4,5},{5,4},{6,7},{7,6},{8,9},{9,8},{10,11... | collective-permute-start | bytes 786440 | tf_op jit(solution)/shard_map/ppermute | solution.py:47
  220.2 7.7 %collective-permute-start.62 = (bf16[128,512]{1,0:T(8,128)(2,1)S(1)}, bf16[128,512]{1,0:T(8,128)(2,1)S(1)}, u32[]{:S(2)}, u32[]{:S(2)}) collective-permute-start(bf16[128,512]{1,0:T(8,128)(2,1)S(1)} %collective-permute-done.49.refs_14_), channel_id=1, source_target_pairs={{0,4},{2,6},{4,0},{6,2},{8,12},{10,14},{12,8},{14,10},{16,20},{18,... | collective-permute-start | bytes 393224 | tf_op jit(solution)/shard_map/ppermute | solution.py:38
  222.1 7.3 %collective-permute-start.60 = (bf16[128,512]{1,0:T(8,128)(2,1)S(1)}, bf16[128,512]{1,0:T(8,128)(2,1)S(1)}, u32[]{:S(2)}, u32[]{:S(2)}) collective-permute-start(bf16[128,512]{1,0:T(8,128)(2,1)S(1)} %collective-permute-done.47.refs_10_), channel_id=1, source_target_pairs={{0,4},{2,6},{4,0},{6,2},{8,12},{10,14},{12,8},{14,10},{16,20},{18,... | collective-permute-start | bytes 393224 | tf_op jit(solution)/shard_map/ppermute | solution.py:38
  222.2 9.0 %collective-permute-start.61 = (bf16[128,512]{1,0:T(8,128)(2,1)S(1)}, bf16[128,512]{1,0:T(8,128)(2,1)S(1)}, u32[]{:S(2)}, u32[]{:S(2)}) collective-permute-start(bf16[128,512]{1,0:T(8,128)(2,1)S(1)} %collective-permute-done.48.refs_12_), channel_id=1, source_target_pairs={{0,4},{2,6},{4,0},{6,2},{8,12},{10,14},{12,8},{14,10},{16,20},{18,... | collective-permute-start | bytes 393224 | tf_op jit(solution)/shard_map/ppermute | solution.py:38
  232.5 2.6 %collective-permute-start.64 = (f32[256,512]{1,0:T(8,128)S(1)}, f32[256,512]{1,0:T(8,128)S(1)}, u32[]{:S(2)}, u32[]{:S(2)}) collective-permute-start(f32[256,512]{1,0:T(8,128)S(1)} %get-tuple-element.99), channel_id=1, source_target_pairs={{0,2},{2,0},{4,6},{6,4},{8,10},{10,8},{12,14},{14,12},{16,18},{18,... | collective-permute-start | bytes 1572872 | tf_op jit(solution)/shard_map/ppermute | solution.py:33
  234.7 6.5 %collective-permute-start.63 = (f32[256,512]{1,0:T(8,128)}, f32[256,512]{1,0:T(8,128)}, u32[]{:S(2)}, u32[]{:S(2)}) collective-permute-start(f32[256,512]{1,0:T(8,128)} %get-tuple-element.97), channel_id=1, source_target_pairs={{0,2},{2,0},{4,6},{6,4},{8,10},{10,8},{12,14},{14,12},{16,18},{18,... | collective-permute-start | bytes 1572872 | tf_op jit(solution)/shard_map/ppermute | solution.py:33
  235.9 8.5 %collective-permute-start.65 = (bf16[256,512]{1,0:T(8,128)(2,1)}, bf16[256,512]{1,0:T(8,128)(2,1)S(1)}, u32[]{:S(2)}, u32[]{:S(2)}) collective-permute-start(bf16[256,512]{1,0:T(8,128)(2,1)} %add_convert_fusion), channel_id=1, source_target_pairs={{0,1},{1,0},{2,3},{3,2},{4,5},{5,4},{6,7},{7,6},{8,9},{9,8},{10,11... | collective-permute-start | bytes 786440 | tf_op jit(solution)/shard_map/ppermute | solution.py:47
  (46 other events, 751.6 us)

commit v2 on v1

--- a/solution.py
+++ b/solution.py
@@ -11,6 +11,7 @@
 KEY_VALUE_HEADS = 8
 HEAD_SIZE = 128
 TILE = 128
+CHUNK = 8
 
 norm_epsilon = 1e-05
 bf16 = jnp.bfloat16
@@ -117,7 +118,7 @@
     size = HEAD_SIZE
     slots = start_ref.shape[1]
     tokens = kv.shape[0] // images
-    span = chunk * tokens
+    unit = 2 if slots % 2 == 0 else 1
     doc = pl.program_id(1)
     rows = group * TILE
 
@@ -136,12 +137,11 @@
     for i in range(slots):
         row = pl.ds(pl.multiple_of(pos_ref[doc, i] * tokens, tokens), tokens)
         here = slice(i * tokens, (i + 1) * tokens)
-        inside = slice(i % chunk * tokens, (i % chunk + 1) * tokens)
         k, v = kv[row, :size], kv[row, size:]
         kc[here, :] = k
         vc[here, :] = v
-        kct[i // chunk, :, inside] = k.T
-        vct[i // chunk, :, inside] = v.T
+        kct[:, here] = k.T
+        vct[:, here] = v.T
 
     def acc_rows(i):
         return pl.ds(pl.multiple_of(pos_ref[doc, i] * tokens, tokens), tokens)
@@ -158,61 +158,62 @@
             n = n + (start_ref[doc, i] < base + TILE).astype(jnp.int32)
         position = base + lax.broadcasted_iota(jnp.int32, (1, rows), 1) % TILE
 
-        def run(chunks):
+        def run(most):
+            cuts = [(i, min(i + chunk, most)) for i in range(0, most, chunk)]
             top = jnp.full((1, rows), -1e30, f32)
             total = jnp.zeros((1, rows), f32)
-            for j in range(chunks):
+            for j, (lo, hi) in enumerate(cuts):
                 s = lax.dot_general(
-                    kc[j * span : (j + 1) * span, :],
+                    kc[lo * tokens : hi * tokens, :],
                     qs[...],
                     (((1,), (1,)), ((), ())),
                     preferred_element_type=f32,
                 )
                 parts = []
-                for i in range(chunk):
-                    hidden = jnp.where(position >= start_ref[doc, chunk * j + i], 0.0, -1e30)
-                    part = s[i * tokens : (i + 1) * tokens] * (scale * math.log2(math.e))
+                for i in range(lo, hi):
+                    hidden = jnp.where(position >= start_ref[doc, i], 0.0, -1e30)
+                    part = s[(i - lo) * tokens :][:tokens] * (scale * math.log2(math.e))
                     parts.append(part + hidden)
                 s = jnp.concatenate(parts, 0)
                 now = jnp.maximum(top, jnp.max(s, axis=0, keepdims=True))
                 e = jnp.exp2(s - now)
-                weights[j] = e
+                weights[lo * tokens : hi * tokens, :] = e
                 tops[j] = now
                 total = total * jnp.exp2(top - now) + jnp.sum(e, axis=0, keepdims=True)
                 top = now
             inverse = 1.0 / total
             turned[...] = jnp.zeros_like(turned)
-            for j in range(chunks):
-                low = (weights[j] * (jnp.exp2(tops[j] - top) * inverse)).astype(bf16)
-                turned[...] += jnp.dot(vct[j], low, preferred_element_type=f32)
+            for j, (lo, hi) in enumerate(cuts):
+                low = (weights[lo * tokens : hi * tokens, :] * (jnp.exp2(tops[j] - top) * inverse)).astype(bf16)
+                turned[...] += jnp.dot(vct[:, lo * tokens : hi * tokens], low, preferred_element_type=f32)
                 dv = jnp.dot(low, gs[...], preferred_element_type=f32)
-                for i in range(chunk):
-                    acc[acc_rows(chunk * j + i), size:] += dv[i * tokens : (i + 1) * tokens]
+                for i in range(lo, hi):
+                    acc[acc_rows(i), size:] += dv[(i - lo) * tokens :][:tokens]
             att = turned[...].astype(bf16)
             for h in range(group):
                 att_ref[here, h * size : (h + 1) * size] = att[:, h * TILE : (h + 1) * TILE].T
             delta = jnp.sum(gt[...].astype(f32) * att.astype(f32), axis=0, keepdims=True)
             turned[...] = jnp.zeros_like(turned)
-            for j in range(chunks):
+            for j, (lo, hi) in enumerate(cuts):
                 dp = lax.dot_general(
-                    vc[j * span : (j + 1) * span, :],
+                    vc[lo * tokens : hi * tokens, :],
                     gs[...],
                     (((1,), (1,)), ((), ())),
                     preferred_element_type=f32,
                 )
-                p = weights[j] * (jnp.exp2(tops[j] - top) * (inverse * scale))
+                p = weights[lo * tokens : hi * tokens, :] * (jnp.exp2(tops[j] - top) * (inverse * scale))
                 ds = (p * (dp - delta)).astype(bf16)
-                turned[...] += jnp.dot(kct[j], ds, preferred_element_type=f32)
+                turned[...] += jnp.dot(kct[:, lo * tokens : hi * tokens], ds, preferred_element_type=f32)
                 dk = jnp.dot(ds, qs[...], preferred_element_type=f32)
-                for i in range(chunk):
-                    acc[acc_rows(chunk * j + i), :size] += dk[i * tokens : (i + 1) * tokens]
+                for i in range(lo, hi):
+                    acc[acc_rows(i), :size] += dk[(i - lo) * tokens :][:tokens]
             dq = turned[...].astype(bf16)
             for h in range(group):
                 dq_ref[here, h * size : (h + 1) * size] = dq[:, h * TILE : (h + 1) * TILE].T
 
-        used = (n + chunk - 1) // chunk
-        for chunks in range(1, slots // chunk + 1):
-            pl.when(used == chunks)(functools.partial(run, chunks))
+        used = (n + unit - 1) // unit
+        for count in range(1, slots // unit + 1):
+            pl.when(used == count)(functools.partial(run, count * unit))
         return carry
 
     lax.fori_loop(0, q_ref.shape[0] // TILE, tile_step, 0)
@@ -236,7 +237,7 @@
     group = span // HEAD_SIZE
     images = lax.axis_size("dp")
     tokens = kv_rows // images
-    chunk = next(c for c in (4, 2, 1) if slots % c == 0)
+    chunk = CHUNK
     rows = group * TILE
     q_spec = pl.BlockSpec((length, span), lambda h, d, *_: (d, h))
     g_spec = pl.BlockSpec((length, span), lambda h, d, *_: (d, heads + h))
@@ -267,10 +268,10 @@
             pltpu.VMEM((kv_rows, 2 * HEAD_SIZE), bf16),
             pltpu.VMEM((slots * tokens, HEAD_SIZE), bf16),
             pltpu.VMEM((slots * tokens, HEAD_SIZE), bf16),
-            pltpu.VMEM((slots // chunk, HEAD_SIZE, chunk * tokens), bf16),
-            pltpu.VMEM((slots // chunk, HEAD_SIZE, chunk * tokens), bf16),
-            pltpu.VMEM((slots // chunk, chunk * tokens, rows), f32),
-            pltpu.VMEM((slots // chunk, 1, rows), f32),
+            pltpu.VMEM((HEAD_SIZE, slots * tokens), bf16),
+            pltpu.VMEM((HEAD_SIZE, slots * tokens), bf16),
+            pltpu.VMEM((slots * tokens, rows), f32),
+            pltpu.VMEM((slots, 1, rows), f32),
             pltpu.VMEM((HEAD_SIZE, rows), f32),
             pltpu.VMEM((kv_rows, 2 * HEAD_SIZE), f32),
         ],

time: 245 us -> 243 us (level)
  starting transfers between devices: 76.8 us -> 67.6 us
  Pallas kernels: 39.6 us -> 42.4 us
    ppermute x20, starting transfers between devices: 36.1 us -> 17.8 us  [swap_x(): return lax.ppermute(a, 'dp', [(i, i ^ 2) for i in range(n)])]
    ppermute x22, starting transfers between devices: 25.2 us -> 32.5 us  [shift_chip(): lax.ppermute(a, 'dp', [(i, (i + 4 * k) % n ^ 2 * r) for i in range(n)])]
    ppermute x22, waiting for transfers between devices: 51.9 us -> 59 us  [shift_chip(): lax.ppermute(a, 'dp', [(i, (i + 4 * k) % n ^ 2 * r) for i in range(n)])]
    ppermute x20, waiting for transfers between devices: 43 us -> 36.5 us  [swap_x(): return lax.ppermute(a, 'dp', [(i, i ^ 2) for i in range(n)])]
    pallas_call x1, Pallas kernels: 24.2 us -> 27.1 us  [attention(): pl.pallas_call(functools.partial(attention_kernel, group, 1.0 / math.sqrt...]
  transfers between devices with their start and end apart: 66 -> 66, of which waited for: 34 -> 36; matrix products, arithmetic and copies ran while one was open for 4% -> 4% of each run, Pallas kernels for 4% -> 4%
where the time goes in v2:
time: 243 us
  waiting for transfers between devices  115 us (47%)
  starting transfers between devices  67.6 us (28%)
  Pallas kernels  42.4 us (17%)
  other arithmetic  8.54 us (4%)
  local copies, waits for them, and re-layouts  7.05 us (3%)
    ppermute x22, waiting for transfers between devices, shift_chip(): lax.ppermute(a, 'dp', [(i, (i + 4 * k) % n ^ 2 * r) for i in range(n)])  59 us
    ppermute x20, waiting for transfers between devices, swap_x(): return lax.ppermute(a, 'dp', [(i, i ^ 2) for i in range(n)])  36.5 us
    ppermute x22, starting transfers between devices, shift_chip(): lax.ppermute(a, 'dp', [(i, (i + 4 * k) % n ^ 2 * r) for i in range(n)])  32.5 us
    pallas_call x1, Pallas kernels, attention(): pl.pallas_call(functools.partial(attention_kernel, group, 1.0 / math.sqrt...  27.1 us
    ppermute x13, waiting for transfers between devices, swap_y(): return lax.ppermute(a, 'sp', [(0, 1), (1, 0)])  18.2 us
    ppermute x20, starting transfers between devices, swap_x(): return lax.ppermute(a, 'dp', [(i, i ^ 2) for i in range(n)])  17.8 us
    pallas_call x14, Pallas kernels, whole_call(): pl.pallas_call(kernel, out_shape=out_shape, in_specs=[smem] * len(scalars...  15.4 us
    ppermute x13, starting transfers between devices, swap_y(): return lax.ppermute(a, 'sp', [(0, 1), (1, 0)])  14.4 us
  transfers between devices with their start and end apart: 66, of which 36 were waited for; matrix products, arithmetic and copies ran while one was open for 4% of the time, Pallas kernels for 4%

profile of v2, /device:TPU:0, one launch (start us, length us, event | category | flops | bytes accessed | tf_op | source)
XLA Modules:
  0.0 243.0 jit_solution(17724938026876337419)
XLA Ops:
  2.1 3.0 %collective-permute-start.5 = (bf16[256,1024]{1,0:T(8,128)(2,1)S(1)}, bf16[256,1024]{1,0:T(8,128)(2,1)S(1)}, u32[]{:S(2)}, u32[]{:S(2)}) collective-permute-start(bf16[256,1024]{1,0:T(8,128)(2,1)S(1)} %pad_maximum_fusion.6), channel_id=1, source_target_pairs={{0,1},{1,0},{2,3},{3,2},{4,5},{5,4},{6,7},{7,6},{8,9},{9,8},{10,11... | collective-permute-start | bytes 1572872 | tf_op jit(solution)/shard_map/ppermute | solution.py:48
  5.9 1.6 collective-permute-start.12
  7.5 2.5 %collective-permute-start.2 = (bf16[128,512]{1,0:T(8,128)(2,1)S(1)}, bf16[128,512]{1,0:T(8,128)(2,1)S(1)}, u32[]{:S(2)}, u32[]{:S(2)}) collective-permute-start(bf16[128,512]{1,0:T(8,128)(2,1)S(1)} %get-tuple-element.109), channel_id=1, source_target_pairs={{0,12},{2,14},{4,8},{6,10},{8,20},{10,22},{12,16},{14,18},{16,28},... | collective-permute-start | bytes 393224 | tf_op jit(solution)/shard_map/ppermute | solution.py:44
  10.0 3.4 %collective-permute-done.12.refs_0_.refs_2_ = bf16[128,512]{1,0:T(8,128)(2,1)S(1)} collective-permute-done((bf16[128,512]{1,0:T(8,128)(2,1)S(1)}, bf16[128,512]{1,0:T(8,128)(2,1)S(1)}, u32[]{:S(2)}, u32[]{:S(2)}) %collective-permute-start.12) | collective-permute-done | bytes 131104 | tf_op jit(solution)/shard_map/ppermute | solution.py:44
  14.1 3.9 %collective-permute-done.2.refs_2_.refs_3_ = bf16[128,512]{1,0:T(8,128)(2,1)S(1)} collective-permute-done((bf16[128,512]{1,0:T(8,128)(2,1)S(1)}, bf16[128,512]{1,0:T(8,128)(2,1)S(1)}, u32[]{:S(2)}, u32[]{:S(2)}) %collective-permute-start.2) | collective-permute-done | bytes 131104 | tf_op jit(solution)/shard_map/ppermute | solution.py:44
  19.6 1.5 collective-permute-start.15
  21.1 3.4 %collective-permute-done.13.refs_0_.refs_4_ = bf16[128,512]{1,0:T(8,128)(2,1)S(1)} collective-permute-done((bf16[128,512]{1,0:T(8,128)(2,1)S(1)}, bf16[128,512]{1,0:T(8,128)(2,1)S(1)}, u32[]{:S(2)}, u32[]{:S(2)}) %collective-permute-start.13) | collective-permute-done | bytes 131104 | tf_op jit(solution)/shard_map/ppermute | solution.py:44
  24.5 2.1 collective-permute-start.14
  26.7 1.6 collective-permute-done.3.refs_2_.refs_5_
  31.1 3.2 %collective-permute-done.4.refs_2_.refs_7_ = bf16[128,512]{1,0:T(8,128)(2,1)S(1)} collective-permute-done((bf16[128,512]{1,0:T(8,128)(2,1)}, bf16[128,512]{1,0:T(8,128)(2,1)S(1)}, u32[]{:S(2)}, u32[]{:S(2)}) %collective-permute-start.4) | collective-permute-done | bytes 131104 | tf_op jit(solution)/shard_map/ppermute | solution.py:44
  35.4 1.5 collective-permute-start.8
  36.9 3.9 %collective-permute-done.16.refs_1_.refs_4_ = bf16[128,512]{1,0:T(8,128)(2,1)S(1)} collective-permute-done((bf16[128,512]{1,0:T(8,128)(2,1)S(1)}, bf16[128,512]{1,0:T(8,128)(2,1)S(1)}, u32[]{:S(2)}, u32[]{:S(2)}) %collective-permute-start.16) | collective-permute-done | bytes 131104 | tf_op jit(solution)/shard_map/ppermute | solution.py:48
  41.2 2.4 collective-permute-done.8.refs_3_.refs_7_
  44.0 3.2 %collective-permute-done.17.refs_1_.refs_6_ = bf16[128,512]{1,0:T(8,128)(2,1)S(1)} collective-permute-done((bf16[128,512]{1,0:T(8,128)(2,1)S(1)}, bf16[128,512]{1,0:T(8,128)(2,1)S(1)}, u32[]{:S(2)}, u32[]{:S(2)}) %collective-permute-start.17) | collective-permute-done | bytes 131104 | tf_op jit(solution)/shard_map/ppermute | solution.py:48
  47.2 1.4 collective-permute-done.9.refs_3_.refs_1_
  49.4 1.7 collective-permute-start.25
  54.2 1.7 collective-permute-start.27
  59.5 3.1 %collective-permute-start.26 = (f16[128,1024]{1,0:T(8,128)(2,1)}, f16[128,1024]{1,0:T(8,128)(2,1)}, u32[]{:S(2)}, u32[]{:S(2)}) collective-permute-start(f16[128,1024]{1,0:T(8,128)(2,1)} %add_convert_fusion.5), channel_id=1, source_target_pairs={{0,24},{2,26},{4,28},{6,30},{8,0},{10,2},{12,4},{14,6},{16,8},{18,... | collective-permute-start | bytes 786440 | tf_op jit(solution)/shard_map/ppermute | solution.py:44
  62.6 1.6 collective-permute-done.23
  65.3 4.6 %collective-permute-done.21 = f16[128,1024]{1,0:T(8,128)(2,1)S(1)} collective-permute-done((f16[128,1024]{1,0:T(8,128)(2,1)S(1)}, f16[128,1024]{1,0:T(8,128)(2,1)S(1)}, u32[]{:S(2)}, u32[]{:S(2)}) %collective-permute-start.21) | collective-permute-done | bytes 262176 | tf_op jit(solution)/shard_map/ppermute | solution.py:39
  71.5 4.6 %collective-permute-done.24 = f16[128,1024]{1,0:T(8,128)(2,1)} collective-permute-done((f16[128,1024]{1,0:T(8,128)(2,1)}, f16[128,1024]{1,0:T(8,128)(2,1)}, u32[]{:S(2)}, u32[]{:S(2)}) %collective-permute-start.24) | collective-permute-done | bytes 262176 | tf_op jit(solution)/shard_map/ppermute | solution.py:44
  76.1 6.9 %collective-permute-done.22 = f16[128,1024]{1,0:T(8,128)(2,1)} collective-permute-done((f16[128,1024]{1,0:T(8,128)(2,1)}, f16[128,1024]{1,0:T(8,128)(2,1)}, u32[]{:S(2)}, u32[]{:S(2)}) %collective-permute-start.22) | collective-permute-done | bytes 262176 | tf_op jit(solution)/shard_map/ppermute | solution.py:44
  83.0 1.4 convert_add_fusion.refs_0_
  85.4 1.4 pad_maximum_fusion
  88.3 3.5 %collective-permute-start.31 = (bf16[256,512]{1,0:T(8,128)(2,1)S(1)}, bf16[256,512]{1,0:T(8,128)(2,1)S(1)}, u32[]{:S(2)}, u32[]{:S(2)}) collective-permute-start(bf16[256,512]{1,0:T(8,128)(2,1)S(1)} %constant_dynamic-update-slice_fusion.refs_2_), channel_id=1, source_target_pairs={{0,24},{2,26},{4,28},{6,30},{8,0},{10,2},{12,4},{14,6},{16,8},{18,... | collective-permute-start | bytes 786440 | tf_op jit(solution)/shard_map/ppermute | solution.py:44
  91.8 6.9 %collective-permute-done.29.refs_3_ = bf16[256,512]{1,0:T(8,128)(2,1)S(1)} collective-permute-done((bf16[256,512]{1,0:T(8,128)(2,1)S(1)}, bf16[256,512]{1,0:T(8,128)(2,1)S(1)}, u32[]{:S(2)}, u32[]{:S(2)}) %collective-permute-start.29) | collective-permute-done | bytes 262176 | tf_op jit(solution)/shard_map/ppermute | solution.py:44
  98.8 1.5 collective-permute-start.32
  100.9 1.5 collective-permute-done.31.refs_5_
  102.3 1.4 collective-permute-start.35
  103.7 5.3 %collective-permute-done.30.refs_4_ = bf16[256,512]{1,0:T(8,128)(2,1)S(1)} collective-permute-done((bf16[256,512]{1,0:T(8,128)(2,1)S(1)}, bf16[256,512]{1,0:T(8,128)(2,1)S(1)}, u32[]{:S(2)}, u32[]{:S(2)}) %collective-permute-start.30) | collective-permute-done | bytes 262176 | tf_op jit(solution)/shard_map/ppermute | solution.py:44
  109.0 1.4 collective-permute-start.34
  110.4 1.4 pad_maximum_fusion.1.refs_0_.refs_1_
  111.8 7.5 %collective-permute-done.35.refs_9_ = bf16[256,512]{1,0:T(8,128)(2,1)S(1)} collective-permute-done((bf16[256,512]{1,0:T(8,128)(2,1)S(1)}, bf16[256,512]{1,0:T(8,128)(2,1)S(1)}, u32[]{:S(2)}, u32[]{:S(2)}) %collective-permute-start.35) | collective-permute-done | bytes 262176 | tf_op jit(solution)/shard_map/ppermute | solution.py:39
  119.3 2.8 %collective-permute-done.34.refs_8_ = bf16[256,512]{1,0:T(8,128)(2,1)S(1)} collective-permute-done((bf16[256,512]{1,0:T(8,128)(2,1)S(1)}, bf16[256,512]{1,0:T(8,128)(2,1)S(1)}, u32[]{:S(2)}, u32[]{:S(2)}) %collective-permute-start.34) | collective-permute-done | bytes 262176 | tf_op jit(solution)/shard_map/ppermute | solution.py:39
  122.2 27.1 %attention.1 = (bf16[512,1024]{1,0:T(8,128)(2,1)S(1)}, bf16[512,1024]{1,0:T(8,128)(2,1)S(1)}, f32[256,512]{1,0:T(8,128)S(1)}, f32[256,512]{1,0:T(8,128)S(1)}, f3...) custom-call(s32[2,16]{1,0:T(2,128)S(1)} %fusion.7.pos_ref, ...), custom_call_target="tpu_custom_call" | custom-call | flops 12884901888 | bytes 9437184 | tf_op jit(solution)/shard_map/attention/pallas_call | solution.py:280
  150.3 2.0 collective-permute-start.40
  152.4 1.9 collective-permute-start.44
  154.5 2.5 %collective-permute-start.37 = (bf16[128,4096]{1,0:T(8,128)(2,1)S(1)}, bf16[128,4096]{1,0:T(8,128)(2,1)S(1)}, u32[]{:S(2)}, u32[]{:S(2)}) collective-permute-start(bf16[128,4096]{1,0:T(8,128)(2,1)S(1)} %pad_maximum_fusion.5), channel_id=1, source_target_pairs={{0,1},{1,0},{2,3},{3,2},{4,5},{5,4},{6,7},{7,6},{8,9},{9,8},{10,11... | collective-permute-start | bytes 3145736 | tf_op jit(solution)/shard_map/ppermute | solution.py:48
  157.0 2.5 %collective-permute-done.38 = bf16[256,512]{1,0:T(8,128)(2,1)S(1)} collective-permute-done((bf16[256,512]{1,0:T(8,128)(2,1)S(1)}, bf16[256,512]{1,0:T(8,128)(2,1)S(1)}, u32[]{:S(2)}, u32[]{:S(2)}) %collective-permute-start.38) | collective-permute-done | bytes 262176 | tf_op jit(solution)/shard_map/ppermute | solution.py:39
  159.7 5.5 %collective-permute-done.40 = bf16[256,512]{1,0:T(8,128)(2,1)S(1)} collective-permute-done((bf16[256,512]{1,0:T(8,128)(2,1)S(1)}, bf16[256,512]{1,0:T(8,128)(2,1)S(1)}, u32[]{:S(2)}, u32[]{:S(2)}) %collective-permute-start.40) | collective-permute-done | bytes 262176 | tf_op jit(solution)/shard_map/ppermute | solution.py:39
  165.2 1.5 collective-permute-start.41
  166.7 4.1 %collective-permute-done.42 = bf16[256,512]{1,0:T(8,128)(2,1)S(1)} collective-permute-done((bf16[256,512]{1,0:T(8,128)(2,1)S(1)}, bf16[256,512]{1,0:T(8,128)(2,1)S(1)}, u32[]{:S(2)}, u32[]{:S(2)}) %collective-permute-start.42) | collective-permute-done | bytes 262176 | tf_op jit(solution)/shard_map/ppermute | solution.py:39
  170.9 6.1 %collective-permute-start.43 = (bf16[256,512]{1,0:T(8,128)(2,1)S(1)}, bf16[256,512]{1,0:T(8,128)(2,1)S(1)}, u32[]{:S(2)}, u32[]{:S(2)}) collective-permute-start(bf16[256,512]{1,0:T(8,128)(2,1)S(1)} %add_convert_fusion.2), channel_id=1, source_target_pairs={{0,24},{2,26},{4,28},{6,30},{8,0},{10,2},{12,4},{14,6},{16,8},{18,... | collective-permute-start | bytes 786440 | tf_op jit(solution)/shard_map/ppermute | solution.py:44
  177.0 3.7 %collective-permute-done.39.refs_1_ = bf16[256,512]{1,0:T(8,128)(2,1)S(1)} collective-permute-done((bf16[256,512]{1,0:T(8,128)(2,1)S(1)}, bf16[256,512]{1,0:T(8,128)(2,1)S(1)}, u32[]{:S(2)}, u32[]{:S(2)}) %collective-permute-start.39) | collective-permute-done | bytes 262176 | tf_op jit(solution)/shard_map/ppermute | solution.py:44
  180.7 3.1 %collective-permute-done.43.refs_3_ = bf16[256,512]{1,0:T(8,128)(2,1)S(1)} collective-permute-done((bf16[256,512]{1,0:T(8,128)(2,1)S(1)}, bf16[256,512]{1,0:T(8,128)(2,1)S(1)}, u32[]{:S(2)}, u32[]{:S(2)}) %collective-permute-start.43) | collective-permute-done | bytes 262176 | tf_op jit(solution)/shard_map/ppermute | solution.py:44
  184.0 1.5 collective-permute-done.45.refs_1_
  186.5 3.2 %collective-permute-start.49 = (bf16[128,512]{1,0:T(8,128)(2,1)S(1)}, bf16[128,512]{1,0:T(8,128)(2,1)S(1)}, u32[]{:S(2)}, u32[]{:S(2)}) collective-permute-start(bf16[128,512]{1,0:T(8,128)(2,1)S(1)} %get-tuple-element.95.refs_8_), channel_id=1, source_target_pairs={{0,24},{2,26},{4,28},{6,30},{8,0},{10,2},{12,4},{14,6},{16,8},{18,... | collective-permute-start | bytes 393224 | tf_op jit(solution)/shard_map/ppermute | solution.py:44
  189.9 3.8 %collective-permute-start.55 = (bf16[128,512]{1,0:T(8,128)(2,1)S(1)}, bf16[128,512]{1,0:T(8,128)(2,1)S(1)}, u32[]{:S(2)}, u32[]{:S(2)}) collective-permute-start(bf16[128,512]{1,0:T(8,128)(2,1)S(1)} %get-tuple-element.90.refs_8_), channel_id=1, source_target_pairs={{0,24},{2,26},{4,28},{6,30},{8,0},{10,2},{12,4},{14,6},{16,8},{18,... | collective-permute-start | bytes 393224 | tf_op jit(solution)/shard_map/ppermute | solution.py:44
  194.1 2.0 collective-permute-done.49.refs_14_
  196.1 3.6 %collective-permute-done.47.refs_10_ = bf16[128,512]{1,0:T(8,128)(2,1)S(1)} collective-permute-done((bf16[128,512]{1,0:T(8,128)(2,1)S(1)}, bf16[128,512]{1,0:T(8,128)(2,1)S(1)}, u32[]{:S(2)}, u32[]{:S(2)}) %collective-permute-start.47) | collective-permute-done | bytes 131104 | tf_op jit(solution)/shard_map/ppermute | solution.py:44
  200.2 1.6 collective-permute-start.56
  201.8 3.6 %collective-permute-done.53.refs_12_ = bf16[128,512]{1,0:T(8,128)(2,1)S(1)} collective-permute-done((bf16[128,512]{1,0:T(8,128)(2,1)S(1)}, bf16[128,512]{1,0:T(8,128)(2,1)S(1)}, u32[]{:S(2)}, u32[]{:S(2)}) %collective-permute-start.53) | collective-permute-done | bytes 131104 | tf_op jit(solution)/shard_map/ppermute | solution.py:44
  205.6 1.8 collective-permute-done.48.refs_12_
  207.4 2.9 %collective-permute-done.54.refs_13_ = bf16[128,512]{1,0:T(8,128)(2,1)S(1)} collective-permute-done((bf16[128,512]{1,0:T(8,128)(2,1)S(1)}, bf16[128,512]{1,0:T(8,128)(2,1)S(1)}, u32[]{:S(2)}, u32[]{:S(2)}) %collective-permute-start.54) | collective-permute-done | bytes 131104 | tf_op jit(solution)/shard_map/ppermute | solution.py:39
  213.7 2.5 %collective-permute-start.59 = (bf16[256,512]{1,0:T(8,128)(2,1)S(1)}, bf16[256,512]{1,0:T(8,128)(2,1)S(1)}, u32[]{:S(2)}, u32[]{:S(2)}) collective-permute-start(bf16[256,512]{1,0:T(8,128)(2,1)S(1)} %add_convert_fusion.1), channel_id=1, source_target_pairs={{0,1},{1,0},{2,3},{3,2},{4,5},{5,4},{6,7},{7,6},{8,9},{9,8},{10,11... | collective-permute-start | bytes 786440 | tf_op jit(solution)/shard_map/ppermute | solution.py:48
  216.5 1.8 collective-permute-start.60
  219.3 3.6 %collective-permute-done.59.refs_2_ = bf16[256,512]{1,0:T(8,128)(2,1)S(1)} collective-permute-done((bf16[256,512]{1,0:T(8,128)(2,1)S(1)}, bf16[256,512]{1,0:T(8,128)(2,1)S(1)}, u32[]{:S(2)}, u32[]{:S(2)}) %collective-permute-start.59) | collective-permute-done | bytes 262176 | tf_op jit(solution)/shard_map/ppermute | solution.py:48
  223.5 1.9 collective-permute-done.60.refs_11_
  225.4 1.7 collective-permute-done.61.refs_13_
  228.5 2.1 weight_gradient.6
  233.5 1.6 place_columns.3
  235.1 1.6 place_columns.2
  236.7 3.7 %collective-permute-done.65.refs_5_ = bf16[256,512]{1,0:T(8,128)(2,1)S(1)} collective-permute-done((bf16[256,512]{1,0:T(8,128)(2,1)}, bf16[256,512]{1,0:T(8,128)(2,1)S(1)}, u32[]{:S(2)}, u32[]{:S(2)}) %collective-permute-start.65) | collective-permute-done | bytes 262176 | tf_op jit(solution)/shard_map/ppermute | solution.py:48
  240.4 2.6 %split_heads.1 = (f32[256,1024]{1,0:T(8,128)}, f32[256,1024]{1,0:T(8,128)}) custom-call(s32[1]{0:T(128)} %bitcast.26.index_ref, f32[256,512]{1,0:T(8,128)S(1)} %copy-done.31, f32[256,512]{1,0:T(8,128)S(1)} %copy-done.33, bf16[256,512]{1,0:T(8,128)(2,1)S(1)} %copy-done.37, f32[256,512]{1,0:T(8,128)S(1)} %copy-done.35, ...), custom_call_target="tpu_custom_call" | custom-call | bytes 4718592 | tf_op jit(solution)/shard_map/split_heads/pallas_call | solution.py:303
  (216 shorter events, 35.0 us)
Async XLA Ops:
  2.1 17.0 %collective-permute-start.5 = (bf16[256,1024]{1,0:T(8,128)(2,1)S(1)}, bf16[256,1024]{1,0:T(8,128)(2,1)S(1)}, u32[]{:S(2)}, u32[]{:S(2)}) collective-permute-start(bf16[256,1024]{1,0:T(8,128)(2,1)S(1)} %pad_maximum_fusion.6), channel_id=1, source_target_pairs={{0,1},{1,0},{2,3},{3,2},{4,5},{5,4},{6,7},{7,6},{8,9},{9,8},{10,11... | collective-permute-start | bytes 1572872 | tf_op jit(solution)/shard_map/ppermute | solution.py:48
  5.9 7.5 %collective-permute-start.12 = (bf16[128,512]{1,0:T(8,128)(2,1)S(1)}, bf16[128,512]{1,0:T(8,128)(2,1)S(1)}, u32[]{:S(2)}, u32[]{:S(2)}) collective-permute-start(bf16[128,512]{1,0:T(8,128)(2,1)S(1)} %get-tuple-element.106), channel_id=1, source_target_pairs={{0,8},{2,10},{4,12},{6,14},{8,16},{10,18},{12,20},{14,22},{16,24},... | collective-permute-start | bytes 393224 | tf_op jit(solution)/shard_map/ppermute | solution.py:44
  7.5 10.5 %collective-permute-start.2 = (bf16[128,512]{1,0:T(8,128)(2,1)S(1)}, bf16[128,512]{1,0:T(8,128)(2,1)S(1)}, u32[]{:S(2)}, u32[]{:S(2)}) collective-permute-start(bf16[128,512]{1,0:T(8,128)(2,1)S(1)} %get-tuple-element.109), channel_id=1, source_target_pairs={{0,12},{2,14},{4,8},{6,10},{8,20},{10,22},{12,16},{14,18},{16,28},... | collective-permute-start | bytes 393224 | tf_op jit(solution)/shard_map/ppermute | solution.py:44
  13.4 11.1 %collective-permute-start.13 = (bf16[128,512]{1,0:T(8,128)(2,1)S(1)}, bf16[128,512]{1,0:T(8,128)(2,1)S(1)}, u32[]{:S(2)}, u32[]{:S(2)}) collective-permute-start(bf16[128,512]{1,0:T(8,128)(2,1)S(1)} %get-tuple-element.61), channel_id=1, source_target_pairs={{0,16},{2,18},{4,20},{6,22},{8,24},{10,26},{12,28},{14,30},{16,0},... | collective-permute-start | bytes 393224 | tf_op jit(solution)/shard_map/ppermute | solution.py:44
  18.0 10.3 %collective-permute-start.3 = (bf16[128,512]{1,0:T(8,128)(2,1)S(1)}, bf16[128,512]{1,0:T(8,128)(2,1)S(1)}, u32[]{:S(2)}, u32[]{:S(2)}) collective-permute-start(bf16[128,512]{1,0:T(8,128)(2,1)S(1)} %get-tuple-element.53), channel_id=1, source_target_pairs={{0,20},{2,22},{4,16},{6,18},{8,28},{10,30},{12,24},{14,26},{16,4},... | collective-permute-start | bytes 393224 | tf_op jit(solution)/shard_map/ppermute | solution.py:44
  19.1 10.2 %collective-permute-start.6 = (bf16[128,512]{1,0:T(8,128)(2,1)S(1)}, bf16[128,512]{1,0:T(8,128)(2,1)S(1)}, u32[]{:S(2)}, u32[]{:S(2)}) collective-permute-start(bf16[128,512]{1,0:T(8,128)(2,1)S(1)} %collective-permute-done.2.refs_2_.refs_3_), channel_id=1, source_target_pairs={{0,1},{1,0},{2,3},{3,2},{4,5},{5,4},{6,7},{7,6},{8,9},{9,8},{10,11... | collective-permute-start | bytes 393224 | tf_op jit(solution)/shard_map/ppermute | solution.py:48
  19.6 10.4 %collective-permute-start.15 = (bf16[128,512]{1,0:T(8,128)(2,1)S(1)}, bf16[128,512]{1,0:T(8,128)(2,1)S(1)}, u32[]{:S(2)}, u32[]{:S(2)}) collective-permute-start(bf16[128,512]{1,0:T(8,128)(2,1)S(1)} %collective-permute-done.12.refs_0_.refs_2_), channel_id=1, source_target_pairs={{0,1},{1,0},{2,3},{3,2},{4,5},{5,4},{6,7},{7,6},{8,9},{9,8},{10,11... | collective-permute-start | bytes 393224 | tf_op jit(solution)/shard_map/ppermute | solution.py:48
  24.5 10.9 %collective-permute-start.14 = (bf16[128,512]{1,0:T(8,128)(2,1)}, bf16[128,512]{1,0:T(8,128)(2,1)S(1)}, u32[]{:S(2)}, u32[]{:S(2)}) collective-permute-start(bf16[128,512]{1,0:T(8,128)(2,1)} %get-tuple-element.62), channel_id=1, source_target_pairs={{0,24},{2,26},{4,28},{6,30},{8,0},{10,2},{12,4},{14,6},{16,8},{18,... | collective-permute-start | bytes 393224 | tf_op jit(solution)/shard_map/ppermute | solution.py:44
  28.3 6.1 %collective-permute-start.4 = (bf16[128,512]{1,0:T(8,128)(2,1)}, bf16[128,512]{1,0:T(8,128)(2,1)S(1)}, u32[]{:S(2)}, u32[]{:S(2)}) collective-permute-start(bf16[128,512]{1,0:T(8,128)(2,1)} %get-tuple-element.54), channel_id=1, source_target_pairs={{0,28},{2,30},{4,24},{6,26},{8,4},{10,6},{12,0},{14,2},{16,12},{18... | collective-permute-start | bytes 393224 | tf_op jit(solution)/shard_map/ppermute | solution.py:44
  29.3 5.5 %collective-permute-start.7 = (bf16[128,512]{1,0:T(8,128)(2,1)S(1)}, bf16[128,512]{1,0:T(8,128)(2,1)S(1)}, u32[]{:S(2)}, u32[]{:S(2)}) collective-permute-start(bf16[128,512]{1,0:T(8,128)(2,1)S(1)} %collective-permute-done.3.refs_2_.refs_5_), channel_id=1, source_target_pairs={{0,1},{1,0},{2,3},{3,2},{4,5},{5,4},{6,7},{7,6},{8,9},{9,8},{10,11... | collective-permute-start | bytes 393224 | tf_op jit(solution)/shard_map/ppermute | solution.py:48
  29.9 18.7 %collective-permute-start.19 = (bf16[256,1024]{1,0:T(8,128)(2,1)S(1)}, bf16[256,1024]{1,0:T(8,128)(2,1)S(1)}, u32[]{:S(2)}, u32[]{:S(2)}) collective-permute-start(bf16[256,1024]{1,0:T(8,128)(2,1)S(1)} %pad_maximum_fusion.7.refs_4_), channel_id=1, source_target_pairs={{0,2},{2,0},{4,6},{6,4},{8,10},{10,8},{12,14},{14,12},{16,18},{18,... | collective-permute-start | bytes 1572872 | tf_op jit(solution)/shard_map/ppermute | solution.py:34
  30.0 18.6 %collective-permute-start.20 = (bf16[256,1024]{1,0:T(8,128)(2,1)S(1)}, bf16[256,1024]{1,0:T(8,128)(2,1)S(1)}, u32[]{:S(2)}, u32[]{:S(2)}) collective-permute-start(bf16[256,1024]{1,0:T(8,128)(2,1)S(1)} %collective-permute-done.5.refs_6_), channel_id=1, source_target_pairs={{0,2},{2,0},{4,6},{6,4},{8,10},{10,8},{12,14},{14,12},{16,18},{18,... | collective-permute-start | bytes 1572872 | tf_op jit(solution)/shard_map/ppermute | solution.py:34
  34.4 6.8 %collective-permute-start.1 = (bf16[128,512]{1,0:T(8,128)(2,1)S(1)}, bf16[128,512]{1,0:T(8,128)(2,1)S(1)}, u32[]{:S(2)}, u32[]{:S(2)}) collective-permute-start(bf16[128,512]{1,0:T(8,128)(2,1)S(1)} %get-tuple-element.112), channel_id=1, source_target_pairs={{0,4},{2,6},{4,0},{6,2},{8,12},{10,14},{12,8},{14,10},{16,20},{18,... | collective-permute-start | bytes 393224 | tf_op jit(solution)/shard_map/ppermute | solution.py:44
  34.9 5.9 %collective-permute-start.16 = (bf16[128,512]{1,0:T(8,128)(2,1)S(1)}, bf16[128,512]{1,0:T(8,128)(2,1)S(1)}, u32[]{:S(2)}, u32[]{:S(2)}) collective-permute-start(bf16[128,512]{1,0:T(8,128)(2,1)S(1)} %collective-permute-done.13.refs_0_.refs_4_), channel_id=1, source_target_pairs={{0,1},{1,0},{2,3},{3,2},{4,5},{5,4},{6,7},{7,6},{8,9},{9,8},{10,11... | collective-permute-start | bytes 393224 | tf_op jit(solution)/shard_map/ppermute | solution.py:48
  35.4 8.2 %collective-permute-start.8 = (bf16[128,512]{1,0:T(8,128)(2,1)S(1)}, bf16[128,512]{1,0:T(8,128)(2,1)S(1)}, u32[]{:S(2)}, u32[]{:S(2)}) collective-permute-start(bf16[128,512]{1,0:T(8,128)(2,1)S(1)} %collective-permute-done.4.refs_2_.refs_7_), channel_id=1, source_target_pairs={{0,1},{1,0},{2,3},{3,2},{4,5},{5,4},{6,7},{7,6},{8,9},{9,8},{10,11... | collective-permute-start | bytes 393224 | tf_op jit(solution)/shard_map/ppermute | solution.py:48
  40.8 6.4 %collective-permute-start.17 = (bf16[128,512]{1,0:T(8,128)(2,1)S(1)}, bf16[128,512]{1,0:T(8,128)(2,1)S(1)}, u32[]{:S(2)}, u32[]{:S(2)}) collective-permute-start(bf16[128,512]{1,0:T(8,128)(2,1)S(1)} %collective-permute-done.14.refs_0_.refs_6_), channel_id=1, source_target_pairs={{0,1},{1,0},{2,3},{3,2},{4,5},{5,4},{6,7},{7,6},{8,9},{9,8},{10,11... | collective-permute-start | bytes 393224 | tf_op jit(solution)/shard_map/ppermute | solution.py:48
  43.6 5.0 %collective-permute-start.9 = (bf16[128,512]{1,0:T(8,128)(2,1)S(1)}, bf16[128,512]{1,0:T(8,128)(2,1)S(1)}, u32[]{:S(2)}, u32[]{:S(2)}) collective-permute-start(bf16[128,512]{1,0:T(8,128)(2,1)S(1)} %collective-permute-done.1.refs_2_.refs_1_), channel_id=1, source_target_pairs={{0,1},{1,0},{2,3},{3,2},{4,5},{5,4},{6,7},{7,6},{8,9},{9,8},{10,11... | collective-permute-start | bytes 393224 | tf_op jit(solution)/shard_map/ppermute | solution.py:48
  47.2 6.2 %collective-permute-start.18 = (bf16[128,512]{1,0:T(8,128)(2,1)S(1)}, bf16[128,512]{1,0:T(8,128)(2,1)S(1)}, u32[]{:S(2)}, u32[]{:S(2)}) collective-permute-start(bf16[128,512]{1,0:T(8,128)(2,1)S(1)} %get-tuple-element.65.refs_0_), channel_id=1, source_target_pairs={{0,1},{1,0},{2,3},{3,2},{4,5},{5,4},{6,7},{7,6},{8,9},{9,8},{10,11... | collective-permute-start | bytes 393224 | tf_op jit(solution)/shard_map/ppermute | solution.py:48
  49.4 9.3 %collective-permute-start.25 = (f16[128,1024]{1,0:T(8,128)(2,1)S(1)}, f16[128,1024]{1,0:T(8,128)(2,1)S(1)}, u32[]{:S(2)}, u32[]{:S(2)}) collective-permute-start(f16[128,1024]{1,0:T(8,128)(2,1)S(1)} %convert_element_type.86), channel_id=1, source_target_pairs={{0,4},{2,6},{4,0},{6,2},{8,12},{10,14},{12,8},{14,10},{16,20},{18,... | collective-permute-start | bytes 786440 | tf_op jit(solution)/shard_map/ppermute | solution.py:39
  52.0 12.3 %collective-permute-start.23 = (f16[128,1024]{1,0:T(8,128)(2,1)S(1)}, f16[128,1024]{1,0:T(8,128)(2,1)S(1)}, u32[]{:S(2)}, u32[]{:S(2)}) collective-permute-start(f16[128,1024]{1,0:T(8,128)(2,1)S(1)} %convert_element_type.82), channel_id=1, source_target_pairs={{0,4},{2,6},{4,0},{6,2},{8,12},{10,14},{12,8},{14,10},{16,20},{18,... | collective-permute-start | bytes 786440 | tf_op jit(solution)/shard_map/ppermute | solution.py:39
  54.2 17.2 %collective-permute-start.27 = (f16[128,1024]{1,0:T(8,128)(2,1)S(1)}, f16[128,1024]{1,0:T(8,128)(2,1)}, u32[]{:S(2)}, u32[]{:S(2)}) collective-permute-start(f16[128,1024]{1,0:T(8,128)(2,1)S(1)} %convert_element_type.90), channel_id=1, source_target_pairs={{0,4},{2,6},{4,0},{6,2},{8,12},{10,14},{12,8},{14,10},{16,20},{18,... | collective-permute-start | bytes 786440 | tf_op jit(solution)/shard_map/ppermute | solution.py:39
  55.9 14.0 %collective-permute-start.21 = (f16[128,1024]{1,0:T(8,128)(2,1)S(1)}, f16[128,1024]{1,0:T(8,128)(2,1)S(1)}, u32[]{:S(2)}, u32[]{:S(2)}) collective-permute-start(f16[128,1024]{1,0:T(8,128)(2,1)S(1)} %convert_element_type.78), channel_id=1, source_target_pairs={{0,4},{2,6},{4,0},{6,2},{8,12},{10,14},{12,8},{14,10},{16,20},{18,... | collective-permute-start | bytes 786440 | tf_op jit(solution)/shard_map/ppermute | solution.py:39
  56.6 28.7 %collective-permute-start.10 = (bf16[128,4096]{1,0:T(8,128)(2,1)S(1)}, bf16[128,4096]{1,0:T(8,128)(2,1)}, u32[]{:S(2)}, u32[]{:S(2)}) collective-permute-start(bf16[128,4096]{1,0:T(8,128)(2,1)S(1)} %pad_maximum_fusion.2), channel_id=1, source_target_pairs={{0,1},{1,0},{2,3},{3,2},{4,5},{5,4},{6,7},{7,6},{8,9},{9,8},{10,11... | collective-permute-start | bytes 3145736 | tf_op jit(solution)/shard_map/ppermute | solution.py:48
  59.5 12.0 %collective-permute-start.26 = (f16[128,1024]{1,0:T(8,128)(2,1)}, f16[128,1024]{1,0:T(8,128)(2,1)}, u32[]{:S(2)}, u32[]{:S(2)}) collective-permute-start(f16[128,1024]{1,0:T(8,128)(2,1)} %add_convert_fusion.5), channel_id=1, source_target_pairs={{0,24},{2,26},{4,28},{6,30},{8,0},{10,2},{12,4},{14,6},{16,8},{18,... | collective-permute-start | bytes 786440 | tf_op jit(solution)/shard_map/ppermute | solution.py:44
  65.0 11.1 %collective-permute-start.24 = (f16[128,1024]{1,0:T(8,128)(2,1)}, f16[128,1024]{1,0:T(8,128)(2,1)}, u32[]{:S(2)}, u32[]{:S(2)}) collective-permute-start(f16[128,1024]{1,0:T(8,128)(2,1)} %add_convert_fusion.6), channel_id=1, source_target_pairs={{0,8},{2,10},{4,12},{6,14},{8,16},{10,18},{12,20},{14,22},{16,24},... | collective-permute-start | bytes 786440 | tf_op jit(solution)/shard_map/ppermute | solution.py:44
  70.6 12.3 %collective-permute-start.22 = (f16[128,1024]{1,0:T(8,128)(2,1)}, f16[128,1024]{1,0:T(8,128)(2,1)}, u32[]{:S(2)}, u32[]{:S(2)}) collective-permute-start(f16[128,1024]{1,0:T(8,128)(2,1)} %add_convert_fusion.7), channel_id=1, source_target_pairs={{0,16},{2,18},{4,20},{6,22},{8,24},{10,26},{12,28},{14,30},{16,0},... | collective-permute-start | bytes 786440 | tf_op jit(solution)/shard_map/ppermute | solution.py:44
  85.3 2.3 collective-permute-start.28
  87.0 23.4 %collective-permute-start.11 = (bf16[256,2048]{1,0:T(8,128)(2,1)S(1)}, bf16[256,2048]{1,0:T(8,128)(2,1)}, u32[]{:S(2)}, u32[]{:S(2)}) collective-permute-start(bf16[256,2048]{1,0:T(8,128)(2,1)S(1)} %pad_maximum_fusion.3), channel_id=1, source_target_pairs={{0,2},{2,0},{4,6},{6,4},{8,10},{10,8},{12,14},{14,12},{16,18},{18,... | collective-permute-start | bytes 3145736 | tf_op jit(solution)/shard_map/ppermute | solution.py:34
  87.7 11.1 %collective-permute-start.29 = (bf16[256,512]{1,0:T(8,128)(2,1)S(1)}, bf16[256,512]{1,0:T(8,128)(2,1)S(1)}, u32[]{:S(2)}, u32[]{:S(2)}) collective-permute-start(bf16[256,512]{1,0:T(8,128)(2,1)S(1)} %constant_dynamic-update-slice_fusion.refs_2_), channel_id=1, source_target_pairs={{0,8},{2,10},{4,12},{6,14},{8,16},{10,18},{12,20},{14,22},{16,24},... | collective-permute-start | bytes 786440 | tf_op jit(solution)/shard_map/ppermute | solution.py:44
  87.9 10.9 %collective-permute-start = (s32[1,2,16]{2,1,0:T(2,128)S(1)}, s32[1,2,16]{2,1,0:T(2,128)S(1)}, u32[]{:S(2)}, u32[]{:S(2)}) collective-permute-start(s32[1,2,16]{2,1,0:T(2,128)S(1)} %bitcast.49), channel_id=1, source_target_pairs={{0,2},{2,0},{4,6},{6,4},{8,10},{10,8},{12,14},{14,12},{16,18},{18,... | collective-permute-start | bytes 392 | tf_op jit(solution)/shard_map/ppermute | solution.py:34
  88.3 14.0 %collective-permute-start.31 = (bf16[256,512]{1,0:T(8,128)(2,1)S(1)}, bf16[256,512]{1,0:T(8,128)(2,1)S(1)}, u32[]{:S(2)}, u32[]{:S(2)}) collective-permute-start(bf16[256,512]{1,0:T(8,128)(2,1)S(1)} %constant_dynamic-update-slice_fusion.refs_2_), channel_id=1, source_target_pairs={{0,24},{2,26},{4,28},{6,30},{8,0},{10,2},{12,4},{14,6},{16,8},{18,... | collective-permute-start | bytes 786440 | tf_op jit(solution)/shard_map/ppermute | solution.py:44
  98.7 10.3 %collective-permute-start.30 = (bf16[256,512]{1,0:T(8,128)(2,1)S(1)}, bf16[256,512]{1,0:T(8,128)(2,1)S(1)}, u32[]{:S(2)}, u32[]{:S(2)}) collective-permute-start(bf16[256,512]{1,0:T(8,128)(2,1)S(1)} %collective-permute-done.29.refs_3_), channel_id=1, source_target_pairs={{0,8},{2,10},{4,12},{6,14},{8,16},{10,18},{12,20},{14,22},{16,24},... | collective-permute-start | bytes 786440 | tf_op jit(solution)/shard_map/ppermute | solution.py:44
  98.8 13.0 %collective-permute-start.32 = (bf16[256,512]{1,0:T(8,128)(2,1)S(1)}, bf16[256,512]{1,0:T(8,128)(2,1)S(1)}, u32[]{:S(2)}, u32[]{:S(2)}) collective-permute-start(bf16[256,512]{1,0:T(8,128)(2,1)S(1)} %constant_dynamic-update-slice_fusion.refs_2_), channel_id=1, source_target_pairs={{0,4},{2,6},{4,0},{6,2},{8,12},{10,14},{12,8},{14,10},{16,20},{18,... | collective-permute-start | bytes 786440 | tf_op jit(solution)/shard_map/ppermute | solution.py:39
  100.2 19.1 %collective-permute-start.33 = (bf16[256,512]{1,0:T(8,128)(2,1)S(1)}, bf16[256,512]{1,0:T(8,128)(2,1)S(1)}, u32[]{:S(2)}, u32[]{:S(2)}) collective-permute-start(bf16[256,512]{1,0:T(8,128)(2,1)S(1)} %collective-permute-done.29.refs_3_), channel_id=1, source_target_pairs={{0,4},{2,6},{4,0},{6,2},{8,12},{10,14},{12,8},{14,10},{16,20},{18,... | collective-permute-start | bytes 786440 | tf_op jit(solution)/shard_map/ppermute | solution.py:39
  102.3 17.0 %collective-permute-start.35 = (bf16[256,512]{1,0:T(8,128)(2,1)S(1)}, bf16[256,512]{1,0:T(8,128)(2,1)S(1)}, u32[]{:S(2)}, u32[]{:S(2)}) collective-permute-start(bf16[256,512]{1,0:T(8,128)(2,1)S(1)} %collective-permute-done.31.refs_5_), channel_id=1, source_target_pairs={{0,4},{2,6},{4,0},{6,2},{8,12},{10,14},{12,8},{14,10},{16,20},{18,... | collective-permute-start | bytes 786440 | tf_op jit(solution)/shard_map/ppermute | solution.py:39
  109.0 13.1 %collective-permute-start.34 = (bf16[256,512]{1,0:T(8,128)(2,1)S(1)}, bf16[256,512]{1,0:T(8,128)(2,1)S(1)}, u32[]{:S(2)}, u32[]{:S(2)}) collective-permute-start(bf16[256,512]{1,0:T(8,128)(2,1)S(1)} %collective-permute-done.30.refs_4_), channel_id=1, source_target_pairs={{0,4},{2,6},{4,0},{6,2},{8,12},{10,14},{12,8},{14,10},{16,20},{18,... | collective-permute-start | bytes 786440 | tf_op jit(solution)/shard_map/ppermute | solution.py:39
  149.4 4.9 %collective-permute-start.36 = (bf16[256,2048]{1,0:T(8,128)(2,1)S(1)}, bf16[256,2048]{1,0:T(8,128)(2,1)S(1)}, u32[]{:S(2)}, u32[]{:S(2)}) collective-permute-start(bf16[256,2048]{1,0:T(8,128)(2,1)S(1)} %pad_maximum_fusion.4), channel_id=1, source_target_pairs={{0,2},{2,0},{4,6},{6,4},{8,10},{10,8},{12,14},{14,12},{16,18},{18,... | collective-permute-start | bytes 3145736 | tf_op jit(solution)/shard_map/ppermute | solution.py:34
  150.2 9.3 %collective-permute-start.38 = (bf16[256,512]{1,0:T(8,128)(2,1)S(1)}, bf16[256,512]{1,0:T(8,128)(2,1)S(1)}, u32[]{:S(2)}, u32[]{:S(2)}) collective-permute-start(bf16[256,512]{1,0:T(8,128)(2,1)S(1)} %get-tuple-element.80), channel_id=1, source_target_pairs={{0,4},{2,6},{4,0},{6,2},{8,12},{10,14},{12,8},{14,10},{16,20},{18,... | collective-permute-start | bytes 786440 | tf_op jit(solution)/shard_map/ppermute | solution.py:39
  150.3 14.8 %collective-permute-start.40 = (bf16[256,512]{1,0:T(8,128)(2,1)S(1)}, bf16[256,512]{1,0:T(8,128)(2,1)S(1)}, u32[]{:S(2)}, u32[]{:S(2)}) collective-permute-start(bf16[256,512]{1,0:T(8,128)(2,1)S(1)} %get-tuple-element.82), channel_id=1, source_target_pairs={{0,4},{2,6},{4,0},{6,2},{8,12},{10,14},{12,8},{14,10},{16,20},{18,... | collective-permute-start | bytes 786440 | tf_op jit(solution)/shard_map/ppermute | solution.py:39
  152.3 18.4 %collective-permute-start.42 = (bf16[256,512]{1,0:T(8,128)(2,1)S(1)}, bf16[256,512]{1,0:T(8,128)(2,1)S(1)}, u32[]{:S(2)}, u32[]{:S(2)}) collective-permute-start(bf16[256,512]{1,0:T(8,128)(2,1)S(1)} %get-tuple-element.84), channel_id=1, source_target_pairs={{0,4},{2,6},{4,0},{6,2},{8,12},{10,14},{12,8},{14,10},{16,20},{18,... | collective-permute-start | bytes 786440 | tf_op jit(solution)/shard_map/ppermute | solution.py:39
  152.4 24.6 %collective-permute-start.44 = (bf16[256,512]{1,0:T(8,128)(2,1)S(1)}, bf16[256,512]{1,0:T(8,128)(2,1)S(1)}, u32[]{:S(2)}, u32[]{:S(2)}) collective-permute-start(bf16[256,512]{1,0:T(8,128)(2,1)S(1)} %get-tuple-element.85), channel_id=1, source_target_pairs={{0,4},{2,6},{4,0},{6,2},{8,12},{10,14},{12,8},{14,10},{16,20},{18,... | collective-permute-start | bytes 786440 | tf_op jit(solution)/shard_map/ppermute | solution.py:39
  154.5 31.3 %collective-permute-start.37 = (bf16[128,4096]{1,0:T(8,128)(2,1)S(1)}, bf16[128,4096]{1,0:T(8,128)(2,1)S(1)}, u32[]{:S(2)}, u32[]{:S(2)}) collective-permute-start(bf16[128,4096]{1,0:T(8,128)(2,1)S(1)} %pad_maximum_fusion.5), channel_id=1, source_target_pairs={{0,1},{1,0},{2,3},{3,2},{4,5},{5,4},{6,7},{7,6},{8,9},{9,8},{10,11... | collective-permute-start | bytes 3145736 | tf_op jit(solution)/shard_map/ppermute | solution.py:48
  159.6 21.1 %collective-permute-start.39 = (bf16[256,512]{1,0:T(8,128)(2,1)S(1)}, bf16[256,512]{1,0:T(8,128)(2,1)S(1)}, u32[]{:S(2)}, u32[]{:S(2)}) collective-permute-start(bf16[256,512]{1,0:T(8,128)(2,1)S(1)} %add_convert_fusion.4), channel_id=1, source_target_pairs={{0,16},{2,18},{4,20},{6,22},{8,24},{10,26},{12,28},{14,30},{16,0},... | collective-permute-start | bytes 786440 | tf_op jit(solution)/shard_map/ppermute | solution.py:44
  165.2 15.5 %collective-permute-start.41 = (bf16[256,512]{1,0:T(8,128)(2,1)S(1)}, bf16[256,512]{1,0:T(8,128)(2,1)S(1)}, u32[]{:S(2)}, u32[]{:S(2)}) collective-permute-start(bf16[256,512]{1,0:T(8,128)(2,1)S(1)} %add_convert_fusion.3), channel_id=1, source_target_pairs={{0,8},{2,10},{4,12},{6,14},{8,16},{10,18},{12,20},{14,22},{16,24},... | collective-permute-start | bytes 786440 | tf_op jit(solution)/shard_map/ppermute | solution.py:44
  170.9 12.9 %collective-permute-start.43 = (bf16[256,512]{1,0:T(8,128)(2,1)S(1)}, bf16[256,512]{1,0:T(8,128)(2,1)S(1)}, u32[]{:S(2)}, u32[]{:S(2)}) collective-permute-start(bf16[256,512]{1,0:T(8,128)(2,1)S(1)} %add_convert_fusion.2), channel_id=1, source_target_pairs={{0,24},{2,26},{4,28},{6,30},{8,0},{10,2},{12,4},{14,6},{16,8},{18,... | collective-permute-start | bytes 786440 | tf_op jit(solution)/shard_map/ppermute | solution.py:44
  185.8 8.2 %collective-permute-start.51 = (bf16[128,512]{1,0:T(8,128)(2,1)S(1)}, bf16[128,512]{1,0:T(8,128)(2,1)S(1)}, u32[]{:S(2)}, u32[]{:S(2)}) collective-permute-start(bf16[128,512]{1,0:T(8,128)(2,1)S(1)} %get-tuple-element.90.refs_8_), channel_id=1, source_target_pairs={{0,8},{2,10},{4,12},{6,14},{8,16},{10,18},{12,20},{14,22},{16,24},... | collective-permute-start | bytes 393224 | tf_op jit(solution)/shard_map/ppermute | solution.py:44
  186.5 9.6 %collective-permute-start.49 = (bf16[128,512]{1,0:T(8,128)(2,1)S(1)}, bf16[128,512]{1,0:T(8,128)(2,1)S(1)}, u32[]{:S(2)}, u32[]{:S(2)}) collective-permute-start(bf16[128,512]{1,0:T(8,128)(2,1)S(1)} %get-tuple-element.95.refs_8_), channel_id=1, source_target_pairs={{0,24},{2,26},{4,28},{6,30},{8,0},{10,2},{12,4},{14,6},{16,8},{18,... | collective-permute-start | bytes 393224 | tf_op jit(solution)/shard_map/ppermute | solution.py:44
  189.7 10.0 %collective-permute-start.47 = (bf16[128,512]{1,0:T(8,128)(2,1)S(1)}, bf16[128,512]{1,0:T(8,128)(2,1)S(1)}, u32[]{:S(2)}, u32[]{:S(2)}) collective-permute-start(bf16[128,512]{1,0:T(8,128)(2,1)S(1)} %get-tuple-element.95.refs_8_), channel_id=1, source_target_pairs={{0,8},{2,10},{4,12},{6,14},{8,16},{10,18},{12,20},{14,22},{16,24},... | collective-permute-start | bytes 393224 | tf_op jit(solution)/shard_map/ppermute | solution.py:44
  189.7 10.0 %collective-permute-start.46 = (bf16[128,512]{1,0:T(8,128)(2,1)S(1)}, bf16[128,512]{1,0:T(8,128)(2,1)S(1)}, u32[]{:S(2)}, u32[]{:S(2)}) collective-permute-start(bf16[128,512]{1,0:T(8,128)(2,1)S(1)} %get-tuple-element.95.refs_8_), channel_id=1, source_target_pairs={{0,4},{2,6},{4,0},{6,2},{8,12},{10,14},{12,8},{14,10},{16,20},{18,... | collective-permute-start | bytes 393224 | tf_op jit(solution)/shard_map/ppermute | solution.py:39
  189.9 10.2 %collective-permute-start.55 = (bf16[128,512]{1,0:T(8,128)(2,1)S(1)}, bf16[128,512]{1,0:T(8,128)(2,1)S(1)}, u32[]{:S(2)}, u32[]{:S(2)}) collective-permute-start(bf16[128,512]{1,0:T(8,128)(2,1)S(1)} %get-tuple-element.90.refs_8_), channel_id=1, source_target_pairs={{0,24},{2,26},{4,28},{6,30},{8,0},{10,2},{12,4},{14,6},{16,8},{18,... | collective-permute-start | bytes 393224 | tf_op jit(solution)/shard_map/ppermute | solution.py:44
  194.1 11.3 %collective-permute-start.53 = (bf16[128,512]{1,0:T(8,128)(2,1)S(1)}, bf16[128,512]{1,0:T(8,128)(2,1)S(1)}, u32[]{:S(2)}, u32[]{:S(2)}) collective-permute-start(bf16[128,512]{1,0:T(8,128)(2,1)S(1)} %collective-permute-done.51.refs_10_), channel_id=1, source_target_pairs={{0,8},{2,10},{4,12},{6,14},{8,16},{10,18},{12,20},{14,22},{16,24},... | collective-permute-start | bytes 393224 | tf_op jit(solution)/shard_map/ppermute | solution.py:44
  196.1 11.3 %collective-permute-start.50 = (bf16[128,512]{1,0:T(8,128)(2,1)S(1)}, bf16[128,512]{1,0:T(8,128)(2,1)S(1)}, u32[]{:S(2)}, u32[]{:S(2)}) collective-permute-start(bf16[128,512]{1,0:T(8,128)(2,1)S(1)} %get-tuple-element.90.refs_8_), channel_id=1, source_target_pairs={{0,4},{2,6},{4,0},{6,2},{8,12},{10,14},{12,8},{14,10},{16,20},{18,... | collective-permute-start | bytes 393224 | tf_op jit(solution)/shard_map/ppermute | solution.py:39
  199.7 7.6 %collective-permute-start.48 = (bf16[128,512]{1,0:T(8,128)(2,1)S(1)}, bf16[128,512]{1,0:T(8,128)(2,1)S(1)}, u32[]{:S(2)}, u32[]{:S(2)}) collective-permute-start(bf16[128,512]{1,0:T(8,128)(2,1)S(1)} %collective-permute-done.47.refs_10_), channel_id=1, source_target_pairs={{0,8},{2,10},{4,12},{6,14},{8,16},{10,18},{12,20},{14,22},{16,24},... | collective-permute-start | bytes 393224 | tf_op jit(solution)/shard_map/ppermute | solution.py:44
  199.7 7.6 %collective-permute-start.52 = (bf16[128,512]{1,0:T(8,128)(2,1)S(1)}, bf16[128,512]{1,0:T(8,128)(2,1)S(1)}, u32[]{:S(2)}, u32[]{:S(2)}) collective-permute-start(bf16[128,512]{1,0:T(8,128)(2,1)S(1)} %collective-permute-done.51.refs_10_), channel_id=1, source_target_pairs={{0,4},{2,6},{4,0},{6,2},{8,12},{10,14},{12,8},{14,10},{16,20},{18,... | collective-permute-start | bytes 393224 | tf_op jit(solution)/shard_map/ppermute | solution.py:39
  200.2 7.2 %collective-permute-start.56 = (bf16[128,512]{1,0:T(8,128)(2,1)S(1)}, bf16[128,512]{1,0:T(8,128)(2,1)S(1)}, u32[]{:S(2)}, u32[]{:S(2)}) collective-permute-start(bf16[128,512]{1,0:T(8,128)(2,1)S(1)} %collective-permute-done.55.refs_14_), channel_id=1, source_target_pairs={{0,4},{2,6},{4,0},{6,2},{8,12},{10,14},{12,8},{14,10},{16,20},{18,... | collective-permute-start | bytes 393224 | tf_op jit(solution)/shard_map/ppermute | solution.py:39
  205.4 5.0 %collective-permute-start.54 = (bf16[128,512]{1,0:T(8,128)(2,1)S(1)}, bf16[128,512]{1,0:T(8,128)(2,1)S(1)}, u32[]{:S(2)}, u32[]{:S(2)}) collective-permute-start(bf16[128,512]{1,0:T(8,128)(2,1)S(1)} %collective-permute-done.53.refs_12_), channel_id=1, source_target_pairs={{0,4},{2,6},{4,0},{6,2},{8,12},{10,14},{12,8},{14,10},{16,20},{18,... | collective-permute-start | bytes 393224 | tf_op jit(solution)/shard_map/ppermute | solution.py:39
  213.1 5.4 %collective-permute-start.57 = (f32[256,512]{1,0:T(8,128)S(1)}, f32[256,512]{1,0:T(8,128)S(1)}, u32[]{:S(2)}, u32[]{:S(2)}) collective-permute-start(f32[256,512]{1,0:T(8,128)S(1)} %get-tuple-element.92), channel_id=1, source_target_pairs={{0,2},{2,0},{4,6},{6,4},{8,10},{10,8},{12,14},{14,12},{16,18},{18,... | collective-permute-start | bytes 1572872 | tf_op jit(solution)/shard_map/ppermute | solution.py:34
  213.7 9.1 %collective-permute-start.59 = (bf16[256,512]{1,0:T(8,128)(2,1)S(1)}, bf16[256,512]{1,0:T(8,128)(2,1)S(1)}, u32[]{:S(2)}, u32[]{:S(2)}) collective-permute-start(bf16[256,512]{1,0:T(8,128)(2,1)S(1)} %add_convert_fusion.1), channel_id=1, source_target_pairs={{0,1},{1,0},{2,3},{3,2},{4,5},{5,4},{6,7},{7,6},{8,9},{9,8},{10,11... | collective-permute-start | bytes 786440 | tf_op jit(solution)/shard_map/ppermute | solution.py:48
  216.2 7.3 %collective-permute-start.62 = (bf16[128,512]{1,0:T(8,128)(2,1)S(1)}, bf16[128,512]{1,0:T(8,128)(2,1)S(1)}, u32[]{:S(2)}, u32[]{:S(2)}) collective-permute-start(bf16[128,512]{1,0:T(8,128)(2,1)S(1)} %collective-permute-done.49.refs_14_), channel_id=1, source_target_pairs={{0,4},{2,6},{4,0},{6,2},{8,12},{10,14},{12,8},{14,10},{16,20},{18,... | collective-permute-start | bytes 393224 | tf_op jit(solution)/shard_map/ppermute | solution.py:39
  216.5 9.0 %collective-permute-start.60 = (bf16[128,512]{1,0:T(8,128)(2,1)S(1)}, bf16[128,512]{1,0:T(8,128)(2,1)S(1)}, u32[]{:S(2)}, u32[]{:S(2)}) collective-permute-start(bf16[128,512]{1,0:T(8,128)(2,1)S(1)} %collective-permute-done.47.refs_10_), channel_id=1, source_target_pairs={{0,4},{2,6},{4,0},{6,2},{8,12},{10,14},{12,8},{14,10},{16,20},{18,... | collective-permute-start | bytes 393224 | tf_op jit(solution)/shard_map/ppermute | solution.py:39
  218.3 8.8 %collective-permute-start.61 = (bf16[128,512]{1,0:T(8,128)(2,1)S(1)}, bf16[128,512]{1,0:T(8,128)(2,1)S(1)}, u32[]{:S(2)}, u32[]{:S(2)}) collective-permute-start(bf16[128,512]{1,0:T(8,128)(2,1)S(1)} %collective-permute-done.48.refs_12_), channel_id=1, source_target_pairs={{0,4},{2,6},{4,0},{6,2},{8,12},{10,14},{12,8},{14,10},{16,20},{18,... | collective-permute-start | bytes 393224 | tf_op jit(solution)/shard_map/ppermute | solution.py:39
  228.4 2.7 %collective-permute-start.64 = (f32[256,512]{1,0:T(8,128)S(1)}, f32[256,512]{1,0:T(8,128)S(1)}, u32[]{:S(2)}, u32[]{:S(2)}) collective-permute-start(f32[256,512]{1,0:T(8,128)S(1)} %get-tuple-element.99), channel_id=1, source_target_pairs={{0,2},{2,0},{4,6},{6,4},{8,10},{10,8},{12,14},{14,12},{16,18},{18,... | collective-permute-start | bytes 1572872 | tf_op jit(solution)/shard_map/ppermute | solution.py:34
  230.5 6.1 %collective-permute-start.63 = (f32[256,512]{1,0:T(8,128)}, f32[256,512]{1,0:T(8,128)}, u32[]{:S(2)}, u32[]{:S(2)}) collective-permute-start(f32[256,512]{1,0:T(8,128)} %get-tuple-element.97), channel_id=1, source_target_pairs={{0,2},{2,0},{4,6},{6,4},{8,10},{10,8},{12,14},{14,12},{16,18},{18,... | collective-permute-start | bytes 1572872 | tf_op jit(solution)/shard_map/ppermute | solution.py:34
  231.8 8.5 %collective-permute-start.65 = (bf16[256,512]{1,0:T(8,128)(2,1)}, bf16[256,512]{1,0:T(8,128)(2,1)S(1)}, u32[]{:S(2)}, u32[]{:S(2)}) collective-permute-start(bf16[256,512]{1,0:T(8,128)(2,1)} %add_convert_fusion), channel_id=1, source_target_pairs={{0,1},{1,0},{2,3},{3,2},{4,5},{5,4},{6,7},{7,6},{8,9},{9,8},{10,11... | collective-permute-start | bytes 786440 | tf_op jit(solution)/shard_map/ppermute | solution.py:48
  (46 other events, 784.2 us)
